TPU v7x, 128 devices: a whole 4x4x4 slice. The times are simulated.
128 devices in a mesh: dp: 32 (over y, x, core), mp: 4 (over z).
Axes of the slice: x: 4, y: 4, z: 4, core: 2. Of those that a mesh axis runs over, the one named last changes fastest.
Arguments:
- gradient: bfloat16 [8, 1024, 28672], P(None, 'dp', 'mp')
- second_moment: bfloat16 [8, 1024, 28672], P(None, 'dp', 'mp'), as said below
- owner_table: int32 [56, 1], replicated, may hold values from 0 to 31; in each aligned block of 56 rows (0 to 55, 56 to 111, ...) at most 3 rows name the same one
- left_roots: bfloat16 [32, 4, 3, 1024, 1024], P('dp', 'mp'), as said below
- right_roots: bfloat16 [32, 4, 3, 1024, 1024], P('dp', 'mp'), as said below
Outputs:
- update: bfloat16 [8, 1024, 28672], P(None, 'dp', 'mp')
Inputs may be any that keep to these rules, and one draw needn't show every extreme that they name: `owner_table`: no index of dp owns more than 3 blocks, some owns exactly 3, and every index owns at least one. `left_roots`: every entry has magnitude below five; no structure is promised. `right_roots`: every entry has magnitude below five; no structure is promised. `second_moment`: Positive.
All inputs are finite; a program needn't handle non-finite values.
Results may differ from a plain program's by a relative error of at most 0.005.
Values may be sent and summed in bfloat16 or wider, within the bound.
No kernel may reach another device: no remote copies, remote signals or barrier semaphores. Data moves between devices by JAX's collectives and lax.ppermute only.
A program may use at most 128 MiB of HBM per device.

v0:
```python
import jax
import jax.numpy as jnp
from jax import lax
from jax.sharding import PartitionSpec as P

beta_two = 0.95
eps_adam = 1e-08
eps_norm = 1e-06


def slot_numbers(owners):
    total_count = owners.shape[0]
    row_ids = lax.broadcasted_iota(jnp.int32, (total_count, total_count), 0)
    others = lax.broadcasted_iota(jnp.int32, (total_count, total_count), 1)
    earlier = (owners[:, None] == owners[None, :]) & (others < row_ids)
    return jnp.sum(earlier.astype(jnp.int32), axis=1)


def precondition(blocks, left_set, rights, squares, block_size):
    left_times = jnp.einsum(
        "sij,sjk->sik", left_set, blocks, preferred_element_type=jnp.float32
    ).astype(jnp.bfloat16)
    product = jnp.einsum("sij,sjk->sik", left_times, rights, preferred_element_type=jnp.float32)
    rms_shampoo = jnp.sqrt(jnp.mean(product * product, axis=(1, 2)) + eps_norm)
    rms_adam = jnp.sqrt(squares / (block_size * block_size) + eps_norm)
    return (product * (rms_adam / rms_shampoo)[:, None, None]).astype(jnp.bfloat16)


def on_device(gradient, second_moment, owner_table, left_roots, right_roots):
    group_size = lax.axis_size("dp")
    my_index = lax.axis_index("dp")
    block_rows, row_count, width = gradient.shape
    block_size = left_roots.shape[-1]
    capacity = left_roots.shape[2]
    block_cols = width // block_size
    block_count = block_rows * block_cols
    owners = owner_table[:, 0]
    slots = slot_numbers(owners)
    target = slots * group_size + owners
    pieces = gradient.reshape(block_rows, row_count, block_cols, block_size)
    pieces = pieces.transpose(0, 2, 1, 3).reshape(block_count, row_count, block_size)
    grad_wide = gradient.astype(jnp.float32)
    moment = beta_two * second_moment.astype(jnp.float32) + (1.0 - beta_two) * grad_wide * grad_wide
    adam_dir = grad_wide / (jnp.sqrt(moment) + eps_adam)
    partial_value = jnp.sum(
        (adam_dir * adam_dir).reshape(block_rows, row_count, block_cols, block_size), axis=(1, 3)
    )
    partial_value = partial_value.reshape(block_count)
    totals = lax.psum(partial_value, "dp")
    slot_ids = lax.broadcasted_iota(jnp.int32, (block_count, capacity), 1)
    is_mine = (owners[:, None] == my_index) & (slots[:, None] == slot_ids)
    squares = jnp.sum(jnp.where(is_mine, totals[:, None], 0.0), axis=0)
    outgoing = (
        jnp.zeros((capacity * group_size, row_count, block_size), jnp.bfloat16)
        .at[target]
        .set(pieces)
    )
    outgoing = outgoing.reshape(capacity, group_size, row_count, block_size)
    received = lax.all_to_all(outgoing, "dp", split_axis=1, concat_axis=1, tiled=True).reshape(
        capacity, block_size, block_size
    )
    left_set = left_roots[0, 0]
    rights = right_roots[0, 0]
    update = precondition(received, left_set, rights, squares, block_size)
    returned = lax.all_to_all(
        update.reshape(capacity, group_size, row_count, block_size),
        "dp",
        split_axis=1,
        concat_axis=1,
        tiled=True,
    )
    own_rows = returned.reshape(capacity * group_size, row_count, block_size)[target]
    own_rows = own_rows.reshape(block_rows, block_cols, row_count, block_size).transpose(0, 2, 1, 3)
    return own_rows.reshape(block_rows, row_count, width)


def solution(mesh):
    return jax.shard_map(
        on_device,
        mesh=mesh,
        in_specs=(
            P(None, "dp", "mp"),
            P(None, "dp", "mp"),
            P(),
            P("dp", "mp", None, None, None),
            P("dp", "mp", None, None, None),
        ),
        out_specs=P(None, "dp", "mp"),
        check_vma=False,
    )
```

profile of v0, /device:TPU:1, one launch (start us, length us, event | category | flops | bytes accessed | tf_op | source)
XLA Modules:
  0.0 307.1 jit_solution(5851420688627000901)
XLA Ops:
  0.0 0.9 convert_reduce_fusion
  0.9 0.7 fusion.16
  1.6 8.1 %reshape.52 = bf16[8,32,7,1024]{3,2,1,0:T(8,128)(2,1)} reshape(bf16[8,32,7168]{2,1,0:T(8,128)(2,1)} %param.5) | data formatting | bytes 7340032 | tf_op jit(solution)/shard_map/reshape | solution.py:40
  9.6 6.4 %copy.21 = bf16[8,7,32,1024]{3,2,1,0:T(8,128)(2,1)} copy(bf16[8,7,32,1024]{3,1,2,0:T(8,128)(2,1)} %bitcast.38) | data formatting | bytes 7340032 | tf_op jit(solution)/shard_map/transpose | solution.py:41
  16.1 3.5 %broadcast_in_dim.20 = bf16[96,32,1024]{2,1,0:T(8,128)(2,1)} broadcast(bf16[]{:T(256)} %constant.12.clone.1), dimensions={} | broadcast | bytes 6291458 | tf_op jit(solution)/shard_map/broadcast_in_dim | solution.py:54
  19.5 11.6 %scatter_fusion = bf16[96,32,1024]{2,1,0:T(8,128)(2,1)} fusion(bf16[96,32,1024]{2,1,0:T(8,128)(2,1)} %broadcast_in_dim.20, s32[56]{0:T(128)S(1)} %fusion.16, bf16[56,32,1024]{2,1,0:T(8,128)(2,1)} %bitcast.41), kind=kCustom, calls=%fused_computation.1 | custom fusion | bytes 11010272 | tf_op jit(solution)/shard_map/scatter | solution.py:56
  31.2 6.8 %copy.22 = bf16[3,32,32,1024]{3,2,0,1:T(8,128)(2,1)} copy(bf16[3,32,32,1024]{3,2,1,0:T(8,128)(2,1)} %bitcast.36) | data formatting | bytes 12582912 | tf_op jit(solution)/shard_map/reshape | solution.py:58
  37.9 8.6 %all-to-all-start = ((bf16[3,32,32,1024]{3,2,0,1:T(8,128)(2,1)}), bf16[3,32,32,1024]{3,2,0,1:T(8,128)(2,1)}, u32[]{:S(2)}, u32[]{:S(2)}) async-start(bf16[3,32,32,1024]{3,2,0,1:T(8,128)(2,1)} %copy.22), calls=%async_computation | async-start | bytes 12582912 | tf_op jit(solution)/shard_map/all_to_all | solution.py:59
  46.6 0.0 copy-start
  46.6 6.7 %fusion.4 = f32[8,7168]{1,0:T(8,128)S(1)} fusion(bf16[8,32,7168]{2,1,0:T(8,128)(2,1)} %param.6, bf16[8,32,7168]{2,1,0:T(8,128)(2,1)} %param.5), kind=kLoop, calls=%fused_computation.10 | loop fusion | flops 18292736 | bytes 7569408 | tf_op jit(solution)/shard_map/reduce_sum | solution.py:45
  53.3 0.1 reduce_sum.46
  53.4 0.1 copy.26
  53.5 0.1 reshape.56
  53.6 120.5 %psum.7 = f32[56]{0:T(128)S(1)} all-reduce(f32[56]{0:T(128)S(1)} %reshape.56), channel_id=1, replica_groups=mesh['dp'=32,'mp'=4] {'dp'}, use_global_device_ids=true, to_apply=%region_4.5 | all-reduce | flops 56 | bytes 448 | tf_op jit(solution)/shard_map/psum | solution.py:49
  174.1 0.1 select_reduce_fusion
  174.2 6.7 %copy.23 = bf16[3,32,32,1024]{3,2,1,0:T(8,128)(2,1)} copy(bf16[3,32,32,1024]{3,2,0,1:T(8,128)(2,1)} %all-to-all-done) | data formatting | bytes 12582912 | tf_op jit(solution)/shard_map/all_to_all | solution.py:59
  181.0 20.2 %multiply_reduce_fusion = (f32[3]{0:T(128)S(1)}, f32[3,1024,1024]{2,1,0:T(8,128)}) fusion(bf16[1,1,3,1024,1024]{4,3,2,1,0:T(8,128)(2,1)} %param.9, bf16[3,1024,1024]{2,1,0:T(8,128)(2,1)} %bitcast.42, bf16[1,1,3,1024,1024]{4,3,2,1,0:T(8,128)(2,1)} %param.8), kind=kOutput, calls=%fused_computation.3 | convolution fusion | flops 12894339072 | bytes 31457292 | tf_op jit(solution)/shard_map/sij,sjk->sik/dot_general | solution.py:23
  201.2 6.6 %multiply_convert_fusion = bf16[3,1024,1024]{2,1,0:T(8,128)(2,1)S(1)} fusion(f32[3,1024,1024]{2,1,0:T(8,128)} %get-tuple-element.6, f32[3]{0:T(128)S(1)} %rsqrt_multiply_fusion), kind=kLoop, calls=%fused_computation.2 | loop fusion | flops 6291456 | bytes 18874380 | tf_op jit(solution)/shard_map/convert_element_type | solution.py:26
  207.8 3.4 %copy.27 = bf16[3,32,32,1024]{3,2,0,1:T(8,128)(2,1)} copy(bf16[3,32,32,1024]{3,2,1,0:T(8,128)(2,1)S(1)} %bitcast.37) | data formatting | bytes 12582912 | tf_op jit(solution)/shard_map/reshape | solution.py:66
  211.1 6.3 %all-to-all-start.1 = ((bf16[3,32,32,1024]{3,2,0,1:T(8,128)(2,1)}), bf16[3,32,32,1024]{3,2,0,1:T(8,128)(2,1)}, u32[]{:S(2)}, u32[]{:S(2)}) async-start(bf16[3,32,32,1024]{3,2,0,1:T(8,128)(2,1)} %copy.27), calls=%async_computation.1 | async-start | bytes 12582912 | tf_op jit(solution)/shard_map/all_to_all | solution.py:65
  217.4 73.0 %all-to-all-done.1 = bf16[3,32,32,1024]{3,2,0,1:T(8,128)(2,1)} async-done(((bf16[3,32,32,1024]{3,2,0,1:T(8,128)(2,1)}), bf16[3,32,32,1024]{3,2,0,1:T(8,128)(2,1)}, u32[]{:S(2)}, u32[]{:S(2)}) %all-to-all-start.1) | async-done | bytes 6291488 | tf_op jit(solution)/shard_map/all_to_all | solution.py:65
  290.4 6.8 %copy.28 = bf16[3,32,32,1024]{3,2,1,0:T(8,128)(2,1)} copy(bf16[3,32,32,1024]{3,2,0,1:T(8,128)(2,1)} %all-to-all-done.1) | data formatting | bytes 12582912 | tf_op jit(solution)/shard_map/all_to_all | solution.py:65
  297.2 5.4 %gather_fusion = bf16[56,32,1024]{2,1,0:T(8,128)(2,1)} fusion(bf16[96,32,1024]{2,1,0:T(8,128)(2,1)} %bitcast.39, s32[1024]{0:T(1024)S(1)} %pad_clamp_fusion), kind=kCustom, calls=%fused_computation | custom fusion | bytes 7340256 | tf_op jit(solution)/shard_map/gather | solution.py:72
  302.6 4.4 %copy.32 = bf16[8,7,4,8,1024]{4,3,1,2,0:T(8,128)(2,1)} copy(bf16[8,7,4,8,1024]{4,3,2,1,0:T(8,128)(2,1)} %bitcast.40) | data formatting | bytes 7340032 | tf_op jit(solution)/shard_map/reshape | solution.py:74
  (5 shorter events, 0.0 us)
Async XLA Ops:
  37.9 136.3 %all-to-all-start = ((bf16[3,32,32,1024]{3,2,0,1:T(8,128)(2,1)}), bf16[3,32,32,1024]{3,2,0,1:T(8,128)(2,1)}, u32[]{:S(2)}, u32[]{:S(2)}) async-start(bf16[3,32,32,1024]{3,2,0,1:T(8,128)(2,1)} %copy.22), calls=%async_computation | async-start | bytes 12582912 | tf_op jit(solution)/shard_map/all_to_all | solution.py:59
  46.6 127.5 %copy-start = (s32[56,1]{0,1:T(1,128)S(1)}, s32[56,1]{0,1:T(1,128)}, u32[]{:S(2)}) copy-start(s32[56,1]{0,1:T(1,128)} %param.7) | copy-start | bytes 676
  211.1 79.3 %all-to-all-start.1 = ((bf16[3,32,32,1024]{3,2,0,1:T(8,128)(2,1)}), bf16[3,32,32,1024]{3,2,0,1:T(8,128)(2,1)}, u32[]{:S(2)}, u32[]{:S(2)}) async-start(bf16[3,32,32,1024]{3,2,0,1:T(8,128)(2,1)} %copy.27), calls=%async_computation.1 | async-start | bytes 12582912 | tf_op jit(solution)/shard_map/all_to_all | solution.py:65
where the time goes:
time: 312 us; the launch traced here: 307 us
  blocking collectives  121 us (39%)
  waiting for transfers between devices  73 us (23%)
  local copies, waits for them, and re-layouts  63.2 us (20%)
  matrix products  20.2 us (6%)
  other arithmetic  15.1 us (5%)
  starting transfers between devices  14.9 us (5%)
    psum x1, blocking collectives, on_device(): totals = lax.psum(partial_value, 'dp')  121 us
    all_to_all x1, waiting for transfers between devices, on_device(): lax.all_to_all(update.reshape(capacity, group_size, row_count, block_size...  73 us
    dot_general x1, matrix products, precondition(): jnp.einsum('sij,sjk->sik', left_times, rights, preferred_element_type=jnp...  20.2 us
    scatter x1, local copies, waits for them, and re-layouts, on_device(): outgoing = jnp.zeros((capacity * group_size, row_count, block_size), jnp....  11.6 us
    all_to_all x1, starting transfers between devices, on_device(): lax.all_to_all(outgoing, 'dp', split_axis=1, concat_axis=1, tiled=True)  8.63 us
    reshape x1, local copies, waits for them, and re-layouts, on_device(): pieces = gradient.reshape(block_rows, row_count, block_cols, block_size)  8.06 us
    reduce_sum x2, other arithmetic, on_device(): jnp.sum((adam_dir * adam_dir).reshape(block_rows, row_count, block_cols,...  6.8 us
    all_to_all x1, local copies, waits for them, and re-layouts, on_device(): lax.all_to_all(update.reshape(capacity, group_size, row_count, block_size...  6.77 us
  transfers between devices with their start and end apart: 2, of which 1 were waited for; matrix products, arithmetic and copies ran while one was open for 2% of the time, Pallas kernels for 0%

commit v1 on v0

v1 whole, which is shorter than its diff:
```python
import functools

import jax
import jax.numpy as jnp
from jax import lax
from jax.experimental import pallas as pl
from jax.experimental.pallas import tpu as pltpu
from jax.sharding import PartitionSpec as P

beta_two = 0.95
eps_adam = 1e-08
eps_norm = 1e-06

TILE = 256
LANES = 128
SUBLANES = 16
IN_HBM = pl.BlockSpec(memory_space=pltpu.HBM)
IN_VMEM = pl.BlockSpec(memory_space=pltpu.VMEM)
IN_SMEM = pl.BlockSpec(memory_space=pltpu.SMEM)


def slot_numbers(owners):
    total_count = owners.shape[0]
    row_ids = lax.broadcasted_iota(jnp.int32, (total_count, total_count), 0)
    others = lax.broadcasted_iota(jnp.int32, (total_count, total_count), 1)
    earlier = (owners[:, None] == owners[None, :]) & (others < row_ids)
    return jnp.sum(earlier.astype(jnp.int32), axis=1)


def pack_kernel(full_slots, owner_ref, grad_ref, send_ref, counts, sems):
    block_rows, row_count, width = grad_ref.shape
    block_size = send_ref.shape[2]
    block_cols = width // block_size
    half = row_count // 2

    def clear(index, carry):
        counts[index] = 0
        return carry

    lax.fori_loop(0, send_ref.shape[0], clear, 0, unroll=8)
    waits = []
    for r in range(block_rows):
        for c in range(block_cols):
            b = r * block_cols + c
            owner = owner_ref[b]
            slot = counts[owner]
            counts[owner] = slot + 1
            columns = pl.ds(c * block_size, block_size)

            @pl.when(slot < full_slots)
            def _():
                start = pl.multiple_of(slot * row_count, row_count)
                pltpu.make_async_copy(
                    grad_ref.at[r, :, columns],
                    send_ref.at[owner, pl.ds(start, row_count), :],
                    sems.at[b],
                ).start()

            if full_slots * row_count < send_ref.shape[1]:
                @pl.when(slot >= full_slots)
                def _():
                    first = 2 * lax.div(owner, 2)
                    for h in range(2):
                        pltpu.make_async_copy(
                            grad_ref.at[r, pl.ds(h * half, half), columns],
                            send_ref.at[first + h, pl.ds(full_slots * row_count, half), :],
                            sems.at[b],
                        ).start()

            waits.append(
                pltpu.make_async_copy(
                    grad_ref.at[r, :, columns], send_ref.at[0, pl.ds(0, row_count), :], sems.at[b]
                )
            )
    for wait in waits:
        wait.wait()


def pack(owners, gradient, group_size, rows, full_slots, block_size):
    return pl.pallas_call(
        functools.partial(pack_kernel, full_slots),
        out_shape=jax.ShapeDtypeStruct((group_size, rows, block_size), jnp.bfloat16),
        in_specs=[IN_SMEM, IN_HBM],
        out_specs=IN_HBM,
        scratch_shapes=[
            pltpu.SMEM((group_size,), jnp.int32),
            pltpu.SemaphoreType.DMA((owners.shape[0],)),
        ],
        compiler_params=pltpu.CompilerParams(vmem_limit_bytes=16 * 2**20),
        cost_estimate=pl.CostEstimate(flops=0, bytes_accessed=4 * gradient.size, transcendentals=0),
    )(owners, gradient)


def three_parts(value):
    high = value.astype(jnp.bfloat16)
    rest = value - high.astype(jnp.float32)
    middle = rest.astype(jnp.bfloat16)
    low = (rest - middle.astype(jnp.float32)).astype(jnp.bfloat16)
    return high, middle, low


def extra_tile(sums, squares):
    rows = lax.broadcasted_iota(jnp.int32, (SUBLANES, LANES), 0)
    content = jnp.zeros((SUBLANES, LANES), jnp.float32)
    for i, part in enumerate([*three_parts(sums), *three_parts(squares)]):
        content = jnp.where(rows == i, part.astype(jnp.float32), content)
    return content.astype(jnp.bfloat16)


def block_product(left_rows, grad, right, times, put):
    count = times.shape[0] // TILE
    for m in range(count):
        times[m * TILE : (m + 1) * TILE, :] = jnp.dot(
            left_rows(m), grad, preferred_element_type=jnp.float32
        ).astype(jnp.bfloat16)
    total = jnp.zeros((8, grad.shape[1]), jnp.float32)
    for m in range(count):
        value = jnp.dot(
            times[m * TILE : (m + 1) * TILE, :], right, preferred_element_type=jnp.float32
        )
        total = total + jnp.sum((value * value).reshape(TILE // 8, 8, -1), axis=0)
        put(m, value.astype(jnp.bfloat16))
    return jnp.sum(jnp.sum(total, axis=0, keepdims=True), axis=1, keepdims=True)


def multiply_kernel(
    slot_count, final, mine_ref, sums_ref, recv_ref, left_ref, right_ref, out_ref, squares_ref,
    grad, times, product, extra, grad_sems, out_sems, extra_sem,
):
    _, group_size, row_count, block_size = grad.shape
    tile_count = block_size // TILE
    per_tile = TILE // row_count
    slot_tiles = product.shape[2]
    lane_tiles = block_size // LANES

    def load(s):
        return pltpu.make_async_copy(
            recv_ref.at[:, pl.ds(s * row_count, row_count), :], grad.at[s], grad_sems.at[s]
        )

    def store(s, m):
        return pltpu.make_async_copy(
            product.at[s, pl.ds(m * per_tile, per_tile)],
            out_ref.at[pl.ds(m * per_tile, per_tile), pl.ds(s * slot_tiles, slot_tiles)],
            out_sems.at[s, m],
        )

    for s in range(slot_count):
        @pl.when(mine_ref[s] >= 0)
        def _():
            load(s).start()

    lane = lax.broadcasted_iota(jnp.int32, (1, LANES), 1)
    squares = jnp.zeros((1, LANES), jnp.float32)
    for s in range(slot_count):
        def compute(s=s):
            load(s).wait()

            def put(m, tile):
                for j in range(lane_tiles):
                    part = tile[:, j * LANES : (j + 1) * LANES].reshape(
                        per_tile, row_count // SUBLANES, SUBLANES, LANES
                    )
                    for h in range(row_count // SUBLANES):
                        product[s, m * per_tile : (m + 1) * per_tile, h * lane_tiles + j] = part[:, h]
                store(s, m).start()

            return block_product(
                lambda m: left_ref[s, m * TILE : (m + 1) * TILE, :],
                grad[s].reshape(block_size, block_size),
                right_ref[s],
                times,
                put,
            )

        value = lax.cond(mine_ref[s] >= 0, compute, lambda: jnp.zeros((1, 1), jnp.float32))
        squares = squares + jnp.where(lane == mine_ref[s], value, 0.0)
    squares_ref[...] = squares

    if final:
        extra[...] = jnp.broadcast_to(
            extra_tile(sums_ref[...], squares)[None, None], extra.shape
        )
        send_extra = pltpu.make_async_copy(
            extra, out_ref.at[:, pl.ds(out_ref.shape[1] - 1, 1)], extra_sem
        )
        send_extra.start()
    for s in range(slot_count):
        @pl.when(mine_ref[s] >= 0)
        def _():
            for m in range(tile_count):
                store(s, m).wait()
    if final:
        send_extra.wait()


def multiply(mine, sums, received, left_set, rights, slot_count, total_tiles, final):
    block_size = left_set.shape[-1]
    group_size = received.shape[0]
    row_count = block_size // group_size
    slot_tiles = row_count * block_size // (SUBLANES * LANES)
    return pl.pallas_call(
        functools.partial(multiply_kernel, slot_count, final),
        out_shape=(
            jax.ShapeDtypeStruct((group_size, total_tiles, SUBLANES, LANES), jnp.bfloat16),
            jax.ShapeDtypeStruct((1, LANES), jnp.float32),
        ),
        in_specs=[IN_SMEM, IN_VMEM, IN_HBM, IN_VMEM, IN_VMEM],
        out_specs=(IN_HBM, IN_VMEM),
        scratch_shapes=[
            pltpu.VMEM((slot_count, group_size, row_count, block_size), jnp.bfloat16),
            pltpu.VMEM((block_size, block_size), jnp.bfloat16),
            pltpu.VMEM((slot_count, group_size, slot_tiles, SUBLANES, LANES), jnp.bfloat16),
            pltpu.VMEM((group_size, 1, SUBLANES, LANES), jnp.bfloat16),
            pltpu.SemaphoreType.DMA((slot_count,)),
            pltpu.SemaphoreType.DMA((slot_count, block_size // TILE)),
            pltpu.SemaphoreType.DMA,
        ],
        compiler_params=pltpu.CompilerParams(vmem_limit_bytes=40 * 2**20),
        cost_estimate=pl.CostEstimate(
            flops=slot_count * 4 * block_size**3,
            bytes_accessed=slot_count * 8 * block_size**2,
            transcendentals=0,
        ),
    )(mine, sums, received, left_set, rights)


def shared_kernel(
    info_ref, sums_ref, squares_ref, own_ref, other_ref, left_ref, right_ref, before_ref, out_ref,
    grad, times, product, extra, grad_sems, out_sems, extra_sem,
):
    group_size, _, half, block_size = grad.shape
    tile_count = times.shape[0] // TILE
    per_tile = TILE // half
    lane_tiles = product.shape[1]
    first_tile = out_ref.shape[1] - 1 - lane_tiles
    block, core = info_ref[0], info_ref[1]
    del before_ref
    loads = [
        pltpu.make_async_copy(own_ref, grad.at[:, core], grad_sems.at[0]),
        pltpu.make_async_copy(other_ref, grad.at[:, 1 - core], grad_sems.at[1]),
    ]

    def store(m):
        return pltpu.make_async_copy(
            product.at[pl.ds(m * per_tile, per_tile)],
            out_ref.at[pl.ds(m * per_tile, per_tile), pl.ds(first_tile, lane_tiles)],
            out_sems.at[m],
        )

    def compute():
        for load in loads:
            load.start()
        for load in loads:
            load.wait()

        def put(m, tile):
            for j in range(lane_tiles):
                product[m * per_tile : (m + 1) * per_tile, j] = tile[
                    :, j * LANES : (j + 1) * LANES
                ].reshape(per_tile, SUBLANES, LANES)
            store(m).start()

        return block_product(
            lambda m: left_ref[m * per_tile : (m + 1) * per_tile].reshape(TILE, block_size),
            grad[...].reshape(block_size, block_size),
            right_ref[...],
            times,
            put,
        )

    value = lax.cond(block >= 0, compute, lambda: jnp.zeros((1, 1), jnp.float32))
    lane = lax.broadcasted_iota(jnp.int32, (1, LANES), 1)
    squares = squares_ref[...] + jnp.where(lane == block, value, 0.0)
    extra[...] = jnp.broadcast_to(extra_tile(sums_ref[...], squares)[None, None], extra.shape)
    send_extra = pltpu.make_async_copy(
        extra, out_ref.at[:, pl.ds(out_ref.shape[1] - 1, 1)], extra_sem
    )
    send_extra.start()

    @pl.when(block >= 0)
    def _():
        for m in range(tile_count):
            store(m).wait()

    send_extra.wait()


def multiply_shared(info, sums, squares, own, other, left_half, right, outgoing):
    group_size, half, block_size = own.shape
    lane_tiles = block_size // LANES
    rows = group_size * half
    return pl.pallas_call(
        shared_kernel,
        out_shape=jax.ShapeDtypeStruct(outgoing.shape, outgoing.dtype),
        in_specs=[IN_SMEM, IN_VMEM, IN_VMEM, IN_HBM, IN_HBM, IN_VMEM, IN_VMEM, IN_HBM],
        out_specs=IN_HBM,
        input_output_aliases={7: 0},
        scratch_shapes=[
            pltpu.VMEM((group_size, 2, half, block_size), jnp.bfloat16),
            pltpu.VMEM((rows, block_size), jnp.bfloat16),
            pltpu.VMEM((group_size, lane_tiles, SUBLANES, LANES), jnp.bfloat16),
            pltpu.VMEM((group_size, 1, SUBLANES, LANES), jnp.bfloat16),
            pltpu.SemaphoreType.DMA((2,)),
            pltpu.SemaphoreType.DMA((rows // TILE,)),
            pltpu.SemaphoreType.DMA,
        ],
        compiler_params=pltpu.CompilerParams(vmem_limit_bytes=32 * 2**20),
        cost_estimate=pl.CostEstimate(
            flops=4 * rows * block_size**2, bytes_accessed=8 * rows * block_size, transcendentals=0
        ),
    )(info, sums, squares, own, other, left_half, right, outgoing)


def unpack_kernel(full_slots, owner_ref, slot_ref, back_ref, out_ref, stage, out_sems):
    block_rows, row_count, width = stage.shape
    block_count = owner_ref.shape[0]
    block_cols = block_count // block_rows
    block_size = width // block_cols
    row_halves = row_count // SUBLANES
    lane_tiles = block_size // LANES
    last = back_ref.shape[1] - 1
    found = jnp.sum(back_ref[:, last].astype(jnp.float32), axis=0)
    count = float(block_size * block_size)
    rms_adam = jnp.sqrt((found[0:1] + found[1:2] + found[2:3]) / count + eps_norm)
    rms_shampoo = jnp.sqrt((found[3:4] + found[4:5] + found[5:6]) / count + eps_norm)
    scale = rms_adam / rms_shampoo
    writes = []
    for r in range(block_rows):
        for c in range(block_cols):
            b = r * block_cols + c
            factor = jnp.broadcast_to(scale[:, b : b + 1], (SUBLANES, LANES))
            owner, slot = owner_ref[b], slot_ref[b]
            for h in range(row_halves):
                whole = slot < full_slots
                source = jnp.where(whole, owner, 2 * lax.div(owner, 2) + h)
                first = jnp.where(
                    whole, (slot * row_halves + h) * lane_tiles, full_slots * row_halves * lane_tiles
                )
                for j in range(lane_tiles):
                    stage[
                        r,
                        h * SUBLANES : (h + 1) * SUBLANES,
                        c * block_size + j * LANES : c * block_size + (j + 1) * LANES,
                    ] = (back_ref[source, first + j].astype(jnp.float32) * factor).astype(jnp.bfloat16)
        write = pltpu.make_async_copy(stage.at[r], out_ref.at[r], out_sems.at[r])
        write.start()
        writes.append(write)
    for write in writes:
        write.wait()


def unpack(owners, slots, back, shape, full_slots):
    block_rows, row_count, width = shape
    return pl.pallas_call(
        functools.partial(unpack_kernel, full_slots),
        out_shape=jax.ShapeDtypeStruct(shape, jnp.bfloat16),
        in_specs=[IN_SMEM, IN_SMEM, IN_VMEM],
        out_specs=IN_HBM,
        scratch_shapes=[
            pltpu.VMEM(shape, jnp.bfloat16),
            pltpu.SemaphoreType.DMA((block_rows,)),
        ],
        compiler_params=pltpu.CompilerParams(vmem_limit_bytes=32 * 2**20),
        cost_estimate=pl.CostEstimate(
            flops=block_rows * row_count * width,
            bytes_accessed=4 * block_rows * row_count * width,
            transcendentals=0,
        ),
    )(owners, slots, back)


def adam_sums(gradient, second_moment, block_cols):
    block_rows, row_count, width = gradient.shape
    grad_wide = gradient.astype(jnp.float32)
    moment = beta_two * second_moment.astype(jnp.float32) + (1.0 - beta_two) * grad_wide * grad_wide
    adam_dir = grad_wide / (jnp.sqrt(moment) + eps_adam)
    sums = jnp.sum(
        (adam_dir * adam_dir).reshape(block_rows, row_count, block_cols, -1), axis=(1, 3)
    ).reshape(1, block_rows * block_cols)
    return jnp.pad(sums, ((0, 0), (0, LANES - block_rows * block_cols)))


def exchange(value):
    return lax.all_to_all(value, "dp", split_axis=0, concat_axis=0, tiled=True)


def on_device(gradient, second_moment, owner_table, left_roots, right_roots):
    group_size = lax.axis_size("dp")
    my_index = lax.axis_index("dp")
    _, row_count, width = gradient.shape
    block_size = left_roots.shape[-1]
    capacity = left_roots.shape[2]
    block_cols = width // block_size
    half = row_count // 2
    lane_tiles = block_size // LANES
    slot_tiles = lane_tiles * (row_count // SUBLANES)
    owners = owner_table[:, 0]
    slots = slot_numbers(owners)
    block_ids = jnp.arange(owners.shape[0], dtype=jnp.int32)
    last_slot = slots == capacity - 1
    both = last_slot[:, None] & last_slot[None, :] & ((owners[:, None] ^ 1) == owners[None, :])

    def mine_at(index, slot):
        return jnp.max(jnp.where((owners == index) & (slots == slot), block_ids, -1))

    def general(gradient, second_moment, left_roots, right_roots):
        send = pack(owners, gradient, group_size, capacity * row_count, capacity, block_size)
        received = exchange(send)
        mine = jnp.stack([mine_at(my_index, s) for s in range(capacity)])
        sums = adam_sums(gradient, second_moment, block_cols)
        outgoing, _ = multiply(
            mine, sums, received, left_roots[0, 0], right_roots[0, 0],
            capacity, capacity * slot_tiles + 1, True,
        )
        return unpack(owners, slots, exchange(outgoing), gradient.shape, capacity)

    def shared(gradient, second_moment, left_roots, right_roots):
        full = capacity - 1
        core = my_index & 1
        partner = [(i, i ^ 1) for i in range(group_size)]
        send = pack(owners, gradient, group_size, full * row_count + half, full, block_size)
        received = exchange(send)
        sums = adam_sums(gradient, second_moment, block_cols)
        mine = jnp.stack([mine_at(my_index, s) for s in range(full)])
        third, other_third = mine_at(my_index, full), mine_at(my_index ^ 1, full)
        info = jnp.stack([jnp.maximum(third, other_third), core])
        left_rows = left_roots[0, 0, full].reshape(group_size, 2, half, block_size)
        left_own = lax.dynamic_index_in_dim(left_rows, core, 1, keepdims=False)
        left_away = lax.dynamic_index_in_dim(left_rows, 1 - core, 1, keepdims=False)
        left_half = jnp.where(
            other_third >= 0, lax.ppermute(left_away, "dp", partner), left_own
        )
        right_own = right_roots[0, 0, full]
        right = jnp.where(other_third >= 0, lax.ppermute(right_own, "dp", partner), right_own)
        own = received[:, full * row_count :, :]
        other = lax.ppermute(own, "dp", partner)
        outgoing, squares = multiply(
            mine, sums, received, left_roots[0, 0], right_roots[0, 0],
            full, full * slot_tiles + lane_tiles + 1, False,
        )
        outgoing = multiply_shared(info, sums, squares, own, other, left_half, right, outgoing)
        return unpack(owners, slots, exchange(outgoing), gradient.shape, full)

    return lax.cond(
        jnp.any(both), general, shared, gradient, second_moment, left_roots, right_roots
    )


def solution(mesh):
    return jax.shard_map(
        on_device,
        mesh=mesh,
        in_specs=(
            P(None, "dp", "mp"),
            P(None, "dp", "mp"),
            P(),
            P("dp", "mp", None, None, None),
            P("dp", "mp", None, None, None),
        ),
        out_specs=P(None, "dp", "mp"),
        check_vma=False,
    )
```

time: 312 us -> 178 us (0.57); the launches traced: 307 us -> 178 us
  local copies, waits for them, and re-layouts: 63.2 us -> 8.81 us
  blocking collectives: 121 us -> 69.6 us
  waiting for transfers between devices: 73 us -> 44.8 us
  Pallas kernels: 0 us -> 23.6 us
  matrix products: 20.2 us -> 0 us
    psum x1 -> x0, blocking collectives: 121 us -> none  [on_device(): totals = lax.psum(partial_value, 'dp')]
    all_to_all x0 -> x1, blocking collectives: none -> 69.6 us  [exchange(): return lax.all_to_all(value, 'dp', split_axis=0, concat_axis=0, tiled=True)]
    all_to_all x2 -> x1, waiting for transfers between devices: 73 us -> 44.8 us  [exchange(): return lax.all_to_all(value, 'dp', split_axis=0, concat_axis=0, tiled=True)]
    pallas_call x0 -> x4, Pallas kernels: none -> 23.6 us  [the longest x1 16.9 us: multiply(): pl.pallas_call(functools.partial(multiply_kernel, slot_count, final), out...]
    reshape x5 -> x1, local copies, waits for them, and re-layouts: 22.7 us -> 0.08 us  [adam_sums(): sums = jnp.sum((adam_dir * adam_dir).reshape(block_rows, row_count, block...]
    dot_general x1 -> x0, matrix products: 20.2 us -> none  [precondition(): jnp.einsum('sij,sjk->sik', left_times, rights, preferred_element_type=jnp...]
    all_to_all x2 -> x0, local copies, waits for them, and re-layouts: 13.5 us -> none  [the longest x1 6.77 us: on_device(): lax.all_to_all(update.reshape(capacity, group_size, row_count, block_size...]
    scatter x1 -> x0, local copies, waits for them, and re-layouts: 11.6 us -> none  [on_device(): outgoing = jnp.zeros((capacity * group_size, row_count, block_size), jnp....]
  transfers between devices with their start and end apart: 2 -> 4, of which waited for: 1 -> 1; matrix products, arithmetic and copies ran while one was open for 2% -> 10% of each run, Pallas kernels for 0% -> 10%
where the time goes in v1:
time: 178 us
  blocking collectives  69.6 us (39%)
  waiting for transfers between devices  44.8 us (25%)
  Pallas kernels  23.6 us (13%)
  starting transfers between devices  13.9 us (8%)
  other arithmetic  13.8 us (8%)
  local copies, waits for them, and re-layouts  8.81 us (5%)
  loops' own time  2.54 us (1%)
    all_to_all x1, blocking collectives, exchange(): return lax.all_to_all(value, 'dp', split_axis=0, concat_axis=0, tiled=True)  69.6 us
    all_to_all x1, waiting for transfers between devices, exchange(): return lax.all_to_all(value, 'dp', split_axis=0, concat_axis=0, tiled=True)  44.8 us
    pallas_call x1, Pallas kernels, multiply(): pl.pallas_call(functools.partial(multiply_kernel, slot_count, final), out...  16.9 us
    all_to_all x1, starting transfers between devices, exchange(): return lax.all_to_all(value, 'dp', split_axis=0, concat_axis=0, tiled=True)  8.64 us
    reduce_sum x2, other arithmetic, adam_sums(): jnp.sum((adam_dir * adam_dir).reshape(block_rows, row_count, block_cols,...  6.83 us
    ppermute x1, starting transfers between devices, shared(): other = lax.ppermute(own, 'dp', partner)  4.63 us
  transfers between devices with their start and end apart: 4, of which 1 were waited for; matrix products, arithmetic and copies ran while one was open for 10% of the time, Pallas kernels for 10%

profile of v1, /device:TPU:1, one launch (start us, length us, event | category | flops | bytes accessed | tf_op | source)
XLA Modules:
  0.0 178.0 jit_solution(13221535088092684169)
XLA Ops:
  0.0 0.9 convert_reduce_fusion
  0.9 0.7 xor_bitcast_fusion
  1.6 1.4 and_reduce_fusion
  3.6 174.1 %conditional.1 = (bf16[8,32,7168]{2,1,0:T(8,128)(2,1)}) conditional(s32[]{:T(128)} %convert_element_type.22, (s32[]{:T(128)}, s32[56]{0:T(128)}, s32[56]{0:T(128)S(1)}, s32[56]{0:T(128)S(1)}, s32[56]{0:T(128)S(1)}, /*index=5*/bf16[8,32,7168]{2,1,0:T(8,128)(2,1)}, bf16[8,32,7168]{2,1,0:T(8,128)(2,1)}, s32[56]{0:T(128)S(1)}, s32[56]{0:T(128)S(1)}, ...), branch_computations={%region_2.9_spmd, %region_9.15_spmd} | conditional | flops 12905088000 | bytes 129700256 | solution.py:445
  3.6 3.4 %branch_0_fun.4 = bf16[32,80,1024]{2,1,0:T(8,128)(2,1)S(1)} custom-call(s32[56]{0:T(128)} %get-tuple-element.7.owner_ref, bf16[8,32,7168]{2,1,0:T(8,128)(2,1)} %get-tuple-element.50.grad_ref), custom_call_target="tpu_custom_call" | custom-call | bytes 7340032 | tf_op jit(solution)/shard_map/cond/branch_0_fun/pallas_call | solution.py:80
  7.0 2.3 %copy-done.1 = bf16[32,80,1024]{2,1,0:T(8,128)(2,1)} copy-done((bf16[32,80,1024]{2,1,0:T(8,128)(2,1)}, bf16[32,80,1024]{2,1,0:T(8,128)(2,1)S(1)}, u32[]{:S(2)}) %copy-start.1) | copy-done | bytes 5242904 | tf_op jit(solution)/shard_map/cond
  9.4 8.6 %all-to-all-start = ((bf16[32,80,1024]{2,1,0:T(8,128)(2,1)}), bf16[32,80,1024]{2,1,0:T(8,128)(2,1)}, u32[]{:S(2)}, u32[]{:S(2)}) async-start(bf16[32,80,1024]{2,1,0:T(8,128)(2,1)} %copy-done.1), calls=%async_computation | async-start | bytes 10485760 | tf_op jit(solution)/shard_map/cond/branch_0_fun/all_to_all | solution.py:385
  18.0 3.1 %slice_bitcast_fusion = bf16[1024,1024]{1,0:T(8,128)(2,1)} fusion(bf16[1,1,3,1024,1024]{4,3,2,1,0:T(8,128)(2,1)} %get-tuple-element.55), kind=kLoop, calls=%fused_computation.7 | loop fusion | bytes 4194304 | tf_op jit(solution)/shard_map/cond/branch_0_fun/squeeze | solution.py:434
  21.1 0.3 collective-permute-start.2
  21.4 1.8 slice.7
  23.2 0.1 dynamic-slice_bitcast_fusion
  23.3 0.3 collective-permute-start.1
  23.6 0.7 fusion.6
  26.2 6.7 %fusion.4 = f32[8,7168]{1,0:T(8,128)S(1)} fusion(bf16[8,32,7168]{2,1,0:T(8,128)(2,1)} %get-tuple-element.51, bf16[8,32,7168]{2,1,0:T(8,128)(2,1)} %get-tuple-element.50.grad_ref), kind=kLoop, calls=%fused_computation.6 | loop fusion | flops 18292736 | bytes 7569408 | tf_op jit(solution)/shard_map/cond/branch_0_fun/reduce_sum | solution.py:378
  33.2 1.3 pad_add_fusion.1.mine_ref
  34.6 0.1 bitcast_select_fusion.left_ref
  34.7 44.8 %all-to-all-done.recv_ref = bf16[32,80,1024]{2,1,0:T(8,128)(2,1)} async-done(((bf16[32,80,1024]{2,1,0:T(8,128)(2,1)}), bf16[32,80,1024]{2,1,0:T(8,128)(2,1)}, u32[]{:S(2)}, u32[]{:S(2)}) %all-to-all-start) | async-done | bytes 5242912 | tf_op jit(solution)/shard_map/cond/branch_0_fun/all_to_all | solution.py:385
  79.5 1.3 slice.9.own_ref
  80.8 4.6 %collective-permute-start = (bf16[32,16,1024]{2,1,0:T(8,128)(2,1)S(1)}, bf16[32,16,1024]{2,1,0:T(8,128)(2,1)S(1)}, u32[]{:S(2)}, u32[]{:S(2)}) collective-permute-start(bf16[32,16,1024]{2,1,0:T(8,128)(2,1)S(1)} %slice.9.own_ref), channel_id=1, source_target_pairs={{0,4},{4,0},{8,12},{12,8},{16,20},{20,16},{24,28},{28,24},{32,36},... | collective-permute-start | bytes 3145736 | tf_op jit(solution)/shard_map/cond/branch_0_fun/ppermute | solution.py:437
  85.5 1.8 %broadcast_select_fusion.right_ref = bf16[1024,1024]{1,0:T(8,128)(2,1)S(1)} fusion(bf16[1024,1024]{1,0:T(8,128)(2,1)} %collective-permute-done.2, pred[]{:T(512)S(6)} %ge.0, bf16[1,1,3,1024,1024]{4,3,2,1,0:T(8,128)(2,1)} %get-tuple-element.55), kind=kLoop, calls=%fused_computation.8 | loop fusion | flops 1048576 | bytes 6291457 | tf_op jit(solution)/shard_map/cond/branch_0_fun/jit(_where)/select_n | solution.py:435
  87.3 16.9 %branch_0_fun.5 = (bf16[32,41,16,128]{3,2,1,0:T(8,128)(2,1)S(1)}, f32[1,128]{1,0:T(1,128)S(1)}) custom-call(s32[2]{0:T(128)S(1)} %pad_add_fusion.1.mine_ref, f32[1,128]{1,0:T(1,128)S(1)} %pad.5.sums_ref, bf16[32,80,1024]{2,1,0:T(8,128)(2,1)} %all-to-all-done.recv_ref, bf16[3,1024,1024]{2,1,0:T(8,128)(2,1)} %bitcast.35, bf16[3,1024,1024]{2,1,0:T(8,128)(2,1)} %bitcast.31), custom_call_target="tpu_custom_call" | custom-call | flops 8589934592 | bytes 16777216 | tf_op jit(solution)/shard_map/cond/branch_0_fun/pallas_call | solution.py:202
  104.2 0.6 branch_0_fun.6
  104.9 69.6 %all_to_all.16.back_ref = bf16[32,41,16,128]{3,2,1,0:T(8,128)(2,1)S(1)} all-to-all(bf16[32,41,16,128]{3,2,1,0:T(8,128)(2,1)S(1)} %branch_0_fun.6), channel_id=1, replica_groups=mesh['dp'=32,'mp'=4] {'dp'}, dimensions={0} | all-to-all | bytes 10747904 | tf_op jit(solution)/shard_map/cond/branch_0_fun/all_to_all | solution.py:385
  174.5 2.7 %branch_0_fun.7 = bf16[8,32,7168]{2,1,0:T(8,128)(2,1)} custom-call(s32[56]{0:T(128)S(1)} %copy-done.2, s32[56]{0:T(128)S(1)} %get-tuple-element.32.slot_ref, bf16[32,41,16,128]{3,2,1,0:T(8,128)(2,1)S(1)} %all_to_all.16.back_ref), custom_call_target="tpu_custom_call" | custom-call | flops 1835008 | bytes 7340032 | tf_op jit(solution)/shard_map/cond/branch_0_fun/pallas_call | solution.py:355
  (14 shorter events, 0.4 us)
Async XLA Ops:
  7.0 2.3 %copy-start.1 = (bf16[32,80,1024]{2,1,0:T(8,128)(2,1)}, bf16[32,80,1024]{2,1,0:T(8,128)(2,1)S(1)}, u32[]{:S(2)}) copy-start(bf16[32,80,1024]{2,1,0:T(8,128)(2,1)S(1)} %branch_0_fun.4) | copy-start | bytes 15728644 | tf_op jit(solution)/shard_map/cond
  9.4 70.1 %all-to-all-start = ((bf16[32,80,1024]{2,1,0:T(8,128)(2,1)}), bf16[32,80,1024]{2,1,0:T(8,128)(2,1)}, u32[]{:S(2)}, u32[]{:S(2)}) async-start(bf16[32,80,1024]{2,1,0:T(8,128)(2,1)} %copy-done.1), calls=%async_computation | async-start | bytes 10485760 | tf_op jit(solution)/shard_map/cond/branch_0_fun/all_to_all | solution.py:385
  18.0 5.6 %copy-start.2 = (s32[56]{0:T(128)S(1)}, s32[56]{0:T(128)}, u32[]{:S(2)}) copy-start(s32[56]{0:T(128)} %get-tuple-element.7.owner_ref) | copy-start | bytes 676 | tf_op jit(solution)/shard_map/cond
  21.1 64.4 %collective-permute-start.2 = (bf16[1024,1024]{1,0:T(8,128)(2,1)}, bf16[1024,1024]{1,0:T(8,128)(2,1)}, u32[]{:S(2)}, u32[]{:S(2)}) collective-permute-start(bf16[1024,1024]{1,0:T(8,128)(2,1)} %slice_bitcast_fusion), channel_id=1, source_target_pairs={{0,4},{4,0},{8,12},{12,8},{16,20},{20,16},{24,28},{28,24},{32,36},... | collective-permute-start | bytes 6291464 | tf_op jit(solution)/shard_map/cond/branch_0_fun/ppermute | solution.py:435
  23.3 11.3 %collective-permute-start.1 = (bf16[32,16,1024]{2,1,0:T(8,128)(2,1)S(1)}, bf16[32,16,1024]{2,1,0:T(8,128)(2,1)}, u32[]{:S(2)}, u32[]{:S(2)}) collective-permute-start(bf16[32,16,1024]{2,1,0:T(8,128)(2,1)S(1)} %dynamic-slice_bitcast_fusion), channel_id=1, source_target_pairs={{0,4},{4,0},{8,12},{12,8},{16,20},{20,16},{24,28},{28,24},{32,36},... | collective-permute-start | bytes 3145736 | tf_op jit(solution)/shard_map/cond/branch_0_fun/ppermute | solution.py:432
  80.8 23.4 %collective-permute-start = (bf16[32,16,1024]{2,1,0:T(8,128)(2,1)S(1)}, bf16[32,16,1024]{2,1,0:T(8,128)(2,1)S(1)}, u32[]{:S(2)}, u32[]{:S(2)}) collective-permute-start(bf16[32,16,1024]{2,1,0:T(8,128)(2,1)S(1)} %slice.9.own_ref), channel_id=1, source_target_pairs={{0,4},{4,0},{8,12},{12,8},{16,20},{20,16},{24,28},{28,24},{32,36},... | collective-permute-start | bytes 3145736 | tf_op jit(solution)/shard_map/cond/branch_0_fun/ppermute | solution.py:437

commit v2 on v1

v2 whole, which is shorter than its diff:
```python
import functools

import jax
import jax.numpy as jnp
from jax import lax
from jax.experimental import pallas as pl
from jax.experimental.pallas import tpu as pltpu
from jax.sharding import PartitionSpec as P

beta_two = 0.95
eps_adam = 1e-08
eps_norm = 1e-06

TILE = 256
LANES = 128
SUBLANES = 16
IN_VMEM = pl.BlockSpec(memory_space=pltpu.VMEM)
IN_SMEM = pl.BlockSpec(memory_space=pltpu.SMEM)
IN_ANY = pl.BlockSpec(memory_space=pl.ANY)


def keep_hbm(*values):
    return [pltpu.with_memory_space_constraint(value, pltpu.HBM) for value in values]


def keep_vmem(*values):
    return [pltpu.with_memory_space_constraint(value, pltpu.VMEM) for value in values]


def pack_kernel(
    full_slots, capacity, first_pass, me_ref, owner_ref, grad_ref, moment_ref, left_ref, right_ref,
    send_ref, sums_ref, slot_ref, info_ref, conflict_ref, left_away, right_away,
    counts, table, stage, moments, partial, stage_sems, away_sems,
):
    block_rows, row_count, width = grad_ref.shape
    group_size, _, block_size = send_ref.shape
    block_cols = width // block_size
    half = row_count // 2
    pairs = [(grad_ref, stage)] + ([(moment_ref, moments)] if first_pass else [])
    loads = [
        [
            pltpu.make_async_copy(source.at[r], target.at[r], stage_sems.at[i, r])
            for i, (source, target) in enumerate(pairs)
        ]
        for r in range(block_rows)
    ]
    for row in loads:
        for load in row:
            load.start()
    me = me_ref[0]
    core = lax.rem(me, 2)
    if first_pass:
        away = [
            pltpu.make_async_copy(left_ref.at[capacity - 1, :, 1 - core], left_away, away_sems.at[0]),
            pltpu.make_async_copy(right_ref.at[capacity - 1], right_away, away_sems.at[1]),
        ]
        for copy in away:
            copy.start()

    for index in range(group_size):
        counts[index] = 0
        for slot in range(capacity):
            table[index * capacity + slot] = -1
    conflict_ref[0] = 0
    partial[...] = jnp.zeros(partial.shape, jnp.float32)

    def block(r, c):
        b = r * block_cols + c
        owner = owner_ref[b]
        slot = counts[owner]
        counts[owner] = slot + 1
        slot_ref[b] = slot
        columns = pl.ds(pl.multiple_of(c * block_size, block_size), block_size)
        shared = slot >= full_slots

        @pl.when(jnp.logical_not(shared))
        def _():
            start = pl.multiple_of(slot * row_count, row_count)
            send_ref[owner, pl.ds(start, row_count), :] = stage[r, :, columns]

        if full_slots < capacity:
            chip = lax.div(owner, 2)
            taken = table[(4 * chip + 1 - owner) * capacity + capacity - 1] >= 0

            @pl.when(shared & taken)
            def _():
                conflict_ref[0] = 1

            @pl.when(shared)
            def _():
                for h in range(2):
                    send_ref[2 * chip + h, pl.ds(full_slots * row_count, half), :] = stage[
                        r, pl.ds(h * half, half), columns
                    ]

        table[owner * capacity + slot] = b
        if first_pass:
            total = jnp.zeros((8, LANES), jnp.float32)
            for k in range(0, block_size, 2 * LANES):
                part = pl.ds(pl.multiple_of(c * block_size + k, 2 * LANES), 2 * LANES)
                wide = stage[r, :, part].astype(jnp.float32)
                moment = beta_two * moments[r, :, part].astype(jnp.float32) + (
                    (1.0 - beta_two) * wide * wide
                )
                direction = wide / (jnp.sqrt(moment) + eps_adam)
                value = jnp.sum((direction * direction).reshape(row_count // 8, 8, -1), axis=0)
                total = total + value[:, :LANES] + value[:, LANES:]
            partial[pl.ds(b, 1), :] = jnp.sum(total, axis=0, keepdims=True)

    for r in range(block_rows):
        for load in loads[r]:
            load.wait()
        lax.fori_loop(0, block_cols, lambda c, carry, r=r: (block(r, c), carry)[1], 0)

    for slot in range(capacity):
        info_ref[slot] = table[me * capacity + slot]
    info_ref[capacity] = table[(me + 1 - 2 * core) * capacity + capacity - 1]
    info_ref[capacity + 1] = core
    sums_ref[...] = lax.dot_general(
        jnp.ones((8, LANES), jnp.float32),
        partial[...],
        (((1,), (1,)), ((), ())),
        precision=lax.Precision.HIGHEST,
        preferred_element_type=jnp.float32,
    )[0:1]
    if first_pass:
        for copy in away:
            copy.wait()


def pack(me, owners, gradient, second_moment, left_set, rights, rows, full_slots):
    first_pass = second_moment is not None
    capacity, group_size, _, half, block_size = left_set.shape
    return pl.pallas_call(
        functools.partial(pack_kernel, full_slots, capacity, first_pass),
        out_shape=(
            pltpu.VMEM((group_size, rows, block_size), jnp.bfloat16),
            jax.ShapeDtypeStruct((1, LANES), jnp.float32),
            jax.ShapeDtypeStruct(owners.shape, jnp.int32),
            jax.ShapeDtypeStruct((capacity + 2,), jnp.int32),
            jax.ShapeDtypeStruct((1,), jnp.int32),
            pltpu.VMEM((group_size, half, block_size), jnp.bfloat16),
            pltpu.VMEM((block_size, block_size), jnp.bfloat16),
        ),
        in_specs=[IN_SMEM, IN_SMEM] + [IN_ANY] * 4,
        out_specs=(IN_VMEM, IN_VMEM, IN_SMEM, IN_SMEM, IN_SMEM, IN_VMEM, IN_VMEM),
        scratch_shapes=[
            pltpu.SMEM((group_size,), jnp.int32),
            pltpu.SMEM((group_size * capacity,), jnp.int32),
            pltpu.VMEM(gradient.shape, jnp.bfloat16),
            pltpu.VMEM(gradient.shape, jnp.bfloat16),
            pltpu.VMEM((LANES, LANES), jnp.float32),
            pltpu.SemaphoreType.DMA((2, gradient.shape[0])),
            pltpu.SemaphoreType.DMA((2,)),
        ],
        compiler_params=pltpu.CompilerParams(vmem_limit_bytes=24 * 2**20),
        cost_estimate=pl.CostEstimate(
            flops=10 * gradient.size, bytes_accessed=8 * gradient.size, transcendentals=2 * gradient.size
        ),
    )(
        me,
        owners,
        *keep_hbm(gradient, second_moment if first_pass else gradient, left_set, rights),
    )


def three_parts(value):
    high = value.astype(jnp.bfloat16)
    rest = value - high.astype(jnp.float32)
    middle = rest.astype(jnp.bfloat16)
    low = (rest - middle.astype(jnp.float32)).astype(jnp.bfloat16)
    return high, middle, low


def extra_tile(sums, squares):
    rows = lax.broadcasted_iota(jnp.int32, (SUBLANES, LANES), 0)
    content = jnp.zeros((SUBLANES, LANES), jnp.float32)
    for i, part in enumerate([*three_parts(sums), *three_parts(squares)]):
        content = jnp.where(rows == i, part.astype(jnp.float32), content)
    return content.astype(jnp.bfloat16)


def block_product(left_rows, grad, right_ready, right, times, put):
    count = times.shape[0] // TILE
    for m in range(count):
        times[m * TILE : (m + 1) * TILE, :] = jnp.dot(
            left_rows(m), grad(), preferred_element_type=jnp.float32
        ).astype(jnp.bfloat16)
    right_ready()
    total = jnp.zeros((8, times.shape[1]), jnp.float32)
    for m in range(count):
        value = jnp.dot(
            times[m * TILE : (m + 1) * TILE, :], right(), preferred_element_type=jnp.float32
        )
        total = total + jnp.sum((value * value).reshape(TILE // 8, 8, -1), axis=0)
        put(m, value.astype(jnp.bfloat16))
    return jnp.sum(jnp.sum(total, axis=0, keepdims=True), axis=1, keepdims=True)


def multiply_kernel(
    slot_count, final, info_ref, sums_ref, recv_ref, left_ref, right_ref,
    out_ref, squares_ref, left_half, right_third, left, right, times, left_sems, right_sems, third_sems,
):
    _, group_size, row_halves, _, block_size = left.shape
    row_count = row_halves * SUBLANES
    tile_count = block_size // TILE
    per_tile = TILE // row_count
    lane_tiles = block_size // LANES
    capacity = left_ref.shape[0]

    def left_load(s, m):
        rows = pl.ds(m * per_tile, per_tile)
        return pltpu.make_async_copy(left_ref.at[s, rows], left.at[s, rows], left_sems.at[s, m])

    def right_load(s):
        return pltpu.make_async_copy(right_ref.at[s], right.at[s], right_sems.at[s])

    for s in range(slot_count):
        @pl.when(info_ref[s] >= 0)
        def _():
            for m in range(tile_count):
                left_load(s, m).start()
            right_load(s).start()

    if not final:
        last = capacity - 1
        own, core = info_ref[last], info_ref[capacity + 1]

        def third_loads():
            return (
                pltpu.make_async_copy(left_ref.at[last, :, core], left_half, third_sems.at[0]),
                pltpu.make_async_copy(right_ref.at[last], right_third, third_sems.at[1]),
            )

        @pl.when(own >= 0)
        def _():
            for load in third_loads():
                load.start()

    lane = lax.broadcasted_iota(jnp.int32, (1, LANES), 1)
    squares = jnp.zeros((1, LANES), jnp.float32)
    for s in range(slot_count):
        def compute(s=s):
            def left_rows(m):
                left_load(s, m).wait()
                return left[s, m * per_tile : (m + 1) * per_tile].reshape(TILE, block_size)

            def put(m, tile):
                for j in range(lane_tiles):
                    part = tile[:, j * LANES : (j + 1) * LANES].reshape(
                        per_tile, row_halves, SUBLANES, LANES
                    )
                    for h in range(row_halves):
                        out_ref[
                            m * per_tile : (m + 1) * per_tile, (s * row_halves + h) * lane_tiles + j
                        ] = part[:, h]

            return block_product(
                left_rows,
                lambda: recv_ref[:, s * row_count : (s + 1) * row_count, :].reshape(
                    block_size, block_size
                ),
                lambda: right_load(s).wait(),
                lambda: right[s],
                times,
                put,
            )

        value = lax.cond(info_ref[s] >= 0, compute, lambda: jnp.zeros((1, 1), jnp.float32))
        squares = squares + jnp.where(lane == info_ref[s], value, 0.0)
    squares_ref[...] = squares

    if final:
        out_ref[:, out_ref.shape[1] - 1] = jnp.broadcast_to(
            extra_tile(sums_ref[...], squares)[None], (group_size, SUBLANES, LANES)
        )
    else:
        @pl.when(own >= 0)
        def _():
            for load in third_loads():
                load.wait()


def multiply(info, sums, received, left_set, rights, slot_count, total_tiles, final):
    capacity, group_size, row_halves, _, block_size = left_set.shape
    return pl.pallas_call(
        functools.partial(multiply_kernel, slot_count, final),
        out_shape=(
            pltpu.VMEM((group_size, total_tiles, SUBLANES, LANES), jnp.bfloat16),
            jax.ShapeDtypeStruct((1, LANES), jnp.float32),
            pltpu.VMEM((group_size, SUBLANES, block_size), jnp.bfloat16),
            pltpu.VMEM((block_size, block_size), jnp.bfloat16),
        ),
        in_specs=[IN_SMEM, IN_VMEM, IN_VMEM, IN_ANY, IN_ANY],
        out_specs=(IN_VMEM,) * 4,
        scratch_shapes=[
            pltpu.VMEM((slot_count, group_size, row_halves, SUBLANES, block_size), jnp.bfloat16),
            pltpu.VMEM((slot_count, block_size, block_size), jnp.bfloat16),
            pltpu.VMEM((block_size, block_size), jnp.bfloat16),
            pltpu.SemaphoreType.DMA((slot_count, block_size // TILE)),
            pltpu.SemaphoreType.DMA((slot_count,)),
            pltpu.SemaphoreType.DMA((2,)),
        ],
        compiler_params=pltpu.CompilerParams(vmem_limit_bytes=(36 if final else 26) * 2**20),
        cost_estimate=pl.CostEstimate(
            flops=slot_count * 4 * block_size**3,
            bytes_accessed=slot_count * 8 * block_size**2,
            transcendentals=0,
        ),
    )(info, sums, *keep_vmem(received), *keep_hbm(left_set, rights))


def shared_kernel(
    info_ref, sums_ref, squares_ref, own_ref, other_ref, left_ref, right_ref, left_away, right_away,
    before_ref, out_ref,
    grad, times, product, extra, grad_sems, out_sems, extra_sem,
):
    group_size, _, half, block_size = grad.shape
    tile_count = times.shape[0] // TILE
    per_tile = TILE // half
    lane_tiles = product.shape[1]
    first_tile = out_ref.shape[1] - 1 - lane_tiles
    capacity = info_ref.shape[0] - 2
    block = jnp.maximum(info_ref[capacity - 1], info_ref[capacity])
    core = info_ref[capacity + 1]
    del before_ref
    loads = [
        pltpu.make_async_copy(own_ref, grad.at[:, core], grad_sems.at[0]),
        pltpu.make_async_copy(other_ref, grad.at[:, 1 - core], grad_sems.at[1]),
    ]

    def store(m):
        return pltpu.make_async_copy(
            product.at[pl.ds(m * per_tile, per_tile)],
            out_ref.at[pl.ds(m * per_tile, per_tile), pl.ds(first_tile, lane_tiles)],
            out_sems.at[m],
        )

    def compute(left_from, right_from):
        for load in loads:
            load.start()
        for load in loads:
            load.wait()

        def put(m, tile):
            for j in range(lane_tiles):
                product[m * per_tile : (m + 1) * per_tile, j] = tile[
                    :, j * LANES : (j + 1) * LANES
                ].reshape(per_tile, SUBLANES, LANES)
            store(m).start()

        return block_product(
            lambda m: left_from[m * per_tile : (m + 1) * per_tile].reshape(TILE, block_size),
            lambda: grad[...].reshape(block_size, block_size),
            lambda: None,
            lambda: right_from[...],
            times,
            put,
        )

    value = lax.cond(
        info_ref[capacity - 1] >= 0,
        lambda: compute(left_ref, right_ref),
        lambda: lax.cond(
            block >= 0,
            lambda: compute(left_away, right_away),
            lambda: jnp.zeros((1, 1), jnp.float32),
        ),
    )
    lane = lax.broadcasted_iota(jnp.int32, (1, LANES), 1)
    squares = squares_ref[...] + jnp.where(lane == block, value, 0.0)
    extra[...] = jnp.broadcast_to(extra_tile(sums_ref[...], squares)[None, None], extra.shape)
    send_extra = pltpu.make_async_copy(
        extra, out_ref.at[:, pl.ds(out_ref.shape[1] - 1, 1)], extra_sem
    )
    send_extra.start()

    @pl.when(block >= 0)
    def _():
        for m in range(tile_count):
            store(m).wait()

    send_extra.wait()


def multiply_shared(
    info, sums, squares, own, other, left_half, right, left_away, right_away, outgoing
):
    group_size, half, block_size = own.shape
    lane_tiles = block_size // LANES
    rows = group_size * half
    return pl.pallas_call(
        shared_kernel,
        out_shape=pltpu.VMEM(outgoing.shape, outgoing.dtype),
        in_specs=[IN_SMEM, IN_VMEM, IN_VMEM, IN_ANY, IN_ANY] + [IN_VMEM] * 4 + [IN_ANY],
        out_specs=IN_ANY,
        input_output_aliases={9: 0},
        scratch_shapes=[
            pltpu.VMEM((group_size, 2, half, block_size), jnp.bfloat16),
            pltpu.VMEM((rows, block_size), jnp.bfloat16),
            pltpu.VMEM((group_size, lane_tiles, SUBLANES, LANES), jnp.bfloat16),
            pltpu.VMEM((group_size, 1, SUBLANES, LANES), jnp.bfloat16),
            pltpu.SemaphoreType.DMA((2,)),
            pltpu.SemaphoreType.DMA((rows // TILE,)),
            pltpu.SemaphoreType.DMA,
        ],
        compiler_params=pltpu.CompilerParams(vmem_limit_bytes=32 * 2**20),
        cost_estimate=pl.CostEstimate(
            flops=4 * rows * block_size**2, bytes_accessed=8 * rows * block_size, transcendentals=0
        ),
    )(
        info, sums, squares,
        *keep_vmem(own, other, left_half, right, left_away, right_away, outgoing),
    )


def unpack_kernel(full_slots, owner_ref, slot_ref, back_ref, out_ref, stage, out_sems):
    block_rows, row_count, width = stage.shape
    block_count = owner_ref.shape[0]
    block_cols = block_count // block_rows
    block_size = width // block_cols
    row_halves = row_count // SUBLANES
    lane_tiles = block_size // LANES
    last = back_ref.shape[1] - 1
    found = jnp.sum(back_ref[:, last].astype(jnp.float32), axis=0)
    count = float(block_size * block_size)
    rms_adam = jnp.sqrt((found[0:1] + found[1:2] + found[2:3]) / count + eps_norm)
    rms_shampoo = jnp.sqrt((found[3:4] + found[4:5] + found[5:6]) / count + eps_norm)
    scale = rms_adam / rms_shampoo
    writes = []
    for r in range(block_rows):
        for c in range(block_cols):
            b = r * block_cols + c
            factor = jnp.broadcast_to(scale[:, b : b + 1], (SUBLANES, LANES))
            owner, slot = owner_ref[b], slot_ref[b]
            for h in range(row_halves):
                whole = slot < full_slots
                source = jnp.where(whole, owner, 2 * lax.div(owner, 2) + h)
                first = jnp.where(
                    whole, (slot * row_halves + h) * lane_tiles, full_slots * row_halves * lane_tiles
                )
                for j in range(lane_tiles):
                    stage[
                        r,
                        h * SUBLANES : (h + 1) * SUBLANES,
                        c * block_size + j * LANES : c * block_size + (j + 1) * LANES,
                    ] = (back_ref[source, first + j].astype(jnp.float32) * factor).astype(jnp.bfloat16)
        write = pltpu.make_async_copy(stage.at[r], out_ref.at[r], out_sems.at[r])
        write.start()
        writes.append(write)
    for write in writes:
        write.wait()


def unpack(owners, slots, back, shape, full_slots):
    block_rows, row_count, width = shape
    return pl.pallas_call(
        functools.partial(unpack_kernel, full_slots),
        out_shape=pltpu.HBM(shape, jnp.bfloat16),
        in_specs=[IN_SMEM, IN_SMEM, IN_VMEM],
        out_specs=IN_ANY,
        scratch_shapes=[
            pltpu.VMEM(shape, jnp.bfloat16),
            pltpu.SemaphoreType.DMA((block_rows,)),
        ],
        compiler_params=pltpu.CompilerParams(vmem_limit_bytes=32 * 2**20),
        cost_estimate=pl.CostEstimate(
            flops=block_rows * row_count * width,
            bytes_accessed=4 * block_rows * row_count * width,
            transcendentals=0,
        ),
    )(owners, slots, *keep_vmem(back))


def exchange(value):
    return lax.all_to_all(value, "dp", split_axis=0, concat_axis=0, tiled=True)


def on_device(gradient, second_moment, owner_table, left_roots, right_roots):
    group_size = lax.axis_size("dp")
    my_index = lax.axis_index("dp")
    _, row_count, width = gradient.shape
    block_size = left_roots.shape[-1]
    capacity = left_roots.shape[2]
    full = capacity - 1
    half = row_count // 2
    lane_tiles = block_size // LANES
    slot_tiles = lane_tiles * (row_count // SUBLANES)
    owners = owner_table[:, 0]
    me = my_index.reshape(1)
    left_set = left_roots.reshape(capacity, group_size, 2, half, block_size)
    rights = right_roots[0, 0]
    send, sums, slots, info, conflict, left_away, right_away = pack(
        me, owners, gradient, second_moment, left_set, rights, full * row_count + half, full
    )

    def general(send, sums, slots, info, left_away, right_away, gradient, left_set, rights):
        send = pack(
            me, owners, gradient, None, left_set, rights, capacity * row_count, capacity
        )[0]
        outgoing = multiply(
            info, sums, exchange(send), left_set, rights, capacity, capacity * slot_tiles + 1, True,
        )[0]
        return unpack(owners, slots, exchange(outgoing), gradient.shape, capacity)

    def shared(send, sums, slots, info, left_away, right_away, gradient, left_set, rights):
        partner = [(i, i ^ 1) for i in range(group_size)]
        received, left_away, right_away = lax.optimization_barrier(
            (exchange(send), left_away, right_away)
        )
        own = received[:, full * row_count :, :]
        other = lax.ppermute(own, "dp", partner)
        left_away = lax.ppermute(left_away, "dp", partner)
        right_away = lax.ppermute(right_away, "dp", partner)
        outgoing, squares, left_half, right_third = multiply(
            info, sums, received, left_set, rights, full, full * slot_tiles + lane_tiles + 1, False,
        )
        outgoing = multiply_shared(
            info, sums, squares, own, other, left_half, right_third, left_away, right_away, outgoing
        )
        return unpack(owners, slots, exchange(outgoing), gradient.shape, full)

    return lax.cond(
        conflict[0] > 0, general, shared,
        send, sums, slots, info, left_away, right_away, gradient, left_set, rights,
    )


def solution(mesh):
    return jax.shard_map(
        on_device,
        mesh=mesh,
        in_specs=(
            P(None, "dp", "mp"),
            P(None, "dp", "mp"),
            P(),
            P("dp", "mp", None, None, None),
            P("dp", "mp", None, None, None),
        ),
        out_specs=P(None, "dp", "mp"),
        check_vma=False,
    )
```

time: 178 us -> 168 us (0.944)
  blocking collectives: 69.6 us -> 140 us
  waiting for transfers between devices: 44.8 us -> 0.01 us
  other arithmetic: 13.8 us -> 0 us
  starting transfers between devices: 13.9 us -> 0.99 us
  local copies, waits for them, and re-layouts: 8.81 us -> 0.1 us
  loops' own time: 2.54 us -> 0.25 us
    all_to_all x1 -> x2, blocking collectives: 69.6 us -> 140 us  [exchange(): return lax.all_to_all(value, 'dp', split_axis=0, concat_axis=0, tiled=True)]
    all_to_all x1 -> x0, waiting for transfers between devices: 44.8 us -> none  [exchange(): return lax.all_to_all(value, 'dp', split_axis=0, concat_axis=0, tiled=True)]
    all_to_all x1 -> x0, starting transfers between devices: 8.64 us -> none  [exchange(): return lax.all_to_all(value, 'dp', split_axis=0, concat_axis=0, tiled=True)]
    reduce_sum x3 -> x0, other arithmetic: 7.73 us -> none  [the longest x2 6.83 us: adam_sums(): jnp.sum((adam_dir * adam_dir).reshape(block_rows, row_count, block_cols,...]
    pallas_call x3, Pallas kernels: 6.66 us -> 12.8 us  [the longest x1 9.49 us: pack(): pl.pallas_call(functools.partial(pack_kernel, full_slots, capacity, first...]
    pallas_call x1, Pallas kernels: 16.9 us -> 12.3 us  [multiply(): pl.pallas_call(functools.partial(multiply_kernel, slot_count, final), out...]
    ppermute x1, starting transfers between devices: 4.63 us -> 0.19 us  [shared(): other = lax.ppermute(own, 'dp', partner)]
    squeeze x2 -> x0, local copies, waits for them, and re-layouts: 3.19 us -> none  [the longest x1 3.09 us: shared(): right_own = right_roots[0, 0, full]]
  transfers between devices with their start and end apart: 4 -> 3, of which waited for: 1 -> 0; matrix products, arithmetic and copies ran while one was open for 10% -> 0% of each run, Pallas kernels for 10% -> 7%
where the time goes in v2:
time: 168 us
  blocking collectives  140 us (83%)
  Pallas kernels  25.1 us (15%)
    all_to_all x2, blocking collectives, exchange(): return lax.all_to_all(value, 'dp', split_axis=0, concat_axis=0, tiled=True)  140 us
    pallas_call x1, Pallas kernels, multiply(): pl.pallas_call(functools.partial(multiply_kernel, slot_count, final), out...  12.3 us
    pallas_call x1, Pallas kernels, pack(): pl.pallas_call(functools.partial(pack_kernel, full_slots, capacity, first...  9.49 us
  transfers between devices with their start and end apart: 3, of which 0 were waited for; matrix products, arithmetic and copies ran while one was open for 0% of the time, Pallas kernels for 7%

profile of v2, /device:TPU:1, one launch (start us, length us, event | category | flops | bytes accessed | tf_op | source)
XLA Modules:
  0.0 167.5 jit_solution(12479476926179130975)
XLA Ops:
  0.0 0.0 copy-start
  0.0 9.5 %shard_map.57 = (bf16[32,80,1024]{2,1,0:T(8,128)(2,1)S(1)}, f32[1,128]{1,0:T(1,128)S(1)}, s32[56]{0:T(128)S(1)}, s32[5]{0:T(128)S(1)}, s32[1]{0:T(128)}, /*index...) custom-call(s32[1]{0:T(128)} %bitcast.me_ref, s32[56]{0:T(128)} %bitcast.11, bf16[8,32,7168]{2,1,0:T(8,128)(2,1)} %grad_ref.1, ...), custom_call_target="tpu_custom_call" | custom-call | flops 18350080 | bytes 14680064 | tf_op jit(solution)/shard_map/pallas_call | solution.py:134
  10.1 0.0 copy-done
  10.2 157.2 %conditional.1 = (bf16[8,32,7168]{2,1,0:T(8,128)(2,1)}) conditional(s32[]{:T(128)} %bitcast.4, (bf16[32,80,1024]{2,1,0:T(8,128)(2,1)S(1)}, bf16[32,16,1024]{2,1,0:T(8,128)(2,1)S(1)}, bf16[1024,1024]{1,0:T(8,128)(2,1)S(1)}, s32[5]{0:T(128)S(1)}, f32[1,128]{1,0:T(1,128)S(1)}, /*index=5*/bf16[3,32,2,16,1024]{4,3,2,1,0:T(8,128)(2,1)}, ...), branch_computations={%region_0.0_spmd, %region_1.0_spmd} | conditional | flops 12905086976 | bytes 72613896 | solution.py:523
  10.2 70.5 %all_to_all.16.recv_ref = bf16[32,80,1024]{2,1,0:T(8,128)(2,1)S(1)} all-to-all(bf16[32,80,1024]{2,1,0:T(8,128)(2,1)S(1)} %get-tuple-element.46), channel_id=1, replica_groups=mesh['dp'=32,'mp'=4] {'dp'}, dimensions={0} | all-to-all | bytes 10485760 | tf_op jit(solution)/shard_map/cond/branch_0_fun/all_to_all | solution.py:476
  80.7 0.4 collective-permute-start.2
  81.1 0.1 slice.2.own_ref
  81.2 0.2 collective-permute-start
  81.4 0.4 collective-permute-start.1
  81.8 12.3 %branch_0_fun.3 = (bf16[32,41,16,128]{3,2,1,0:T(8,128)(2,1)S(1)}, f32[1,128]{1,0:T(1,128)S(1)}, bf16[32,16,1024]{2,1,0:T(8,128)(2,1)S(1)}, bf16[1024,1024]{1,0:T(8,128)(2,1)S(1)}) custom-call(s32[5]{0:T(128)S(1)} %get-tuple-element.44.info_ref, f32[1,128]{1,0:T(1,128)S(1)} %get-tuple-element.45.sums_ref, bf16[32,80,1024]{2,1,0:T(8,128)(2,1)S(1)} %all_to_all.16.recv_ref, ...), custom_call_target="tpu_custom_call" | custom-call | flops 8589934592 | bytes 16777216 | tf_op jit(solution)/shard_map/cond/branch_0_fun/pallas_call | solution.py:286
  94.1 0.0 collective-permute-done.other_ref
  94.1 0.0 collective-permute-done.1.left_away
  94.1 0.0 collective-permute-done.2.right_away
  94.1 0.6 branch_0_fun.4
  94.7 69.8 %all_to_all.17.back_ref = bf16[32,41,16,128]{3,2,1,0:T(8,128)(2,1)S(1)} all-to-all(bf16[32,41,16,128]{3,2,1,0:T(8,128)(2,1)S(1)} %branch_0_fun.4), channel_id=1, replica_groups=mesh['dp'=32,'mp'=4] {'dp'}, dimensions={0} | all-to-all | bytes 10747904 | tf_op jit(solution)/shard_map/cond/branch_0_fun/all_to_all | solution.py:476
  164.5 2.7 %branch_0_fun.5 = bf16[8,32,7168]{2,1,0:T(8,128)(2,1)} custom-call(s32[56]{0:T(128)S(1)} %get-tuple-element.42.owner_ref, s32[56]{0:T(128)S(1)} %get-tuple-element.43.slot_ref, bf16[32,41,16,128]{3,2,1,0:T(8,128)(2,1)S(1)} %all_to_all.17.back_ref), custom_call_target="tpu_custom_call" | custom-call | flops 1835008 | bytes 7340032 | tf_op jit(solution)/shard_map/cond/branch_0_fun/pallas_call | solution.py:457
Async XLA Ops:
  0.0 10.2 %copy-start = (s32[56,1]{0,1:T(1,128)S(1)}, s32[56,1]{0,1:T(1,128)}, u32[]{:S(2)}) copy-start(s32[56,1]{0,1:T(1,128)} %param.9) | copy-start | bytes 676
  80.7 13.4 %collective-permute-start.2 = (bf16[1024,1024]{1,0:T(8,128)(2,1)S(1)}, bf16[1024,1024]{1,0:T(8,128)(2,1)S(1)}, u32[]{:S(2)}, u32[]{:S(2)}) collective-permute-start(bf16[1024,1024]{1,0:T(8,128)(2,1)S(1)} %get-tuple-element.56), channel_id=1, source_target_pairs={{0,4},{4,0},{8,12},{12,8},{16,20},{20,16},{24,28},{28,24},{32,36},... | collective-permute-start | bytes 6291464 | tf_op jit(solution)/shard_map/cond/branch_0_fun/ppermute | solution.py:514
  81.2 12.9 %collective-permute-start = (bf16[32,16,1024]{2,1,0:T(8,128)(2,1)S(1)}, bf16[32,16,1024]{2,1,0:T(8,128)(2,1)S(1)}, u32[]{:S(2)}, u32[]{:S(2)}) collective-permute-start(bf16[32,16,1024]{2,1,0:T(8,128)(2,1)S(1)} %slice.2.own_ref), channel_id=1, source_target_pairs={{0,4},{4,0},{8,12},{12,8},{16,20},{20,16},{24,28},{28,24},{32,36},... | collective-permute-start | bytes 3145736 | tf_op jit(solution)/shard_map/cond/branch_0_fun/ppermute | solution.py:512
  81.4 12.7 %collective-permute-start.1 = (bf16[32,16,1024]{2,1,0:T(8,128)(2,1)S(1)}, bf16[32,16,1024]{2,1,0:T(8,128)(2,1)S(1)}, u32[]{:S(2)}, u32[]{:S(2)}) collective-permute-start(bf16[32,16,1024]{2,1,0:T(8,128)(2,1)S(1)} %get-tuple-element.55), channel_id=1, source_target_pairs={{0,4},{4,0},{8,12},{12,8},{16,20},{20,16},{24,28},{28,24},{32,36},... | collective-permute-start | bytes 3145736 | tf_op jit(solution)/shard_map/cond/branch_0_fun/ppermute | solution.py:513

commit v3 on v2

--- a/solution.py
+++ b/solution.py
@@ -72,27 +72,15 @@
         slot_ref[b] = slot
         columns = pl.ds(pl.multiple_of(c * block_size, block_size), block_size)
         shared = slot >= full_slots
-
-        @pl.when(jnp.logical_not(shared))
-        def _():
-            start = pl.multiple_of(slot * row_count, row_count)
-            send_ref[owner, pl.ds(start, row_count), :] = stage[r, :, columns]
-
-        if full_slots < capacity:
-            chip = lax.div(owner, 2)
-            taken = table[(4 * chip + 1 - owner) * capacity + capacity - 1] >= 0
-
-            @pl.when(shared & taken)
-            def _():
-                conflict_ref[0] = 1
-
-            @pl.when(shared)
-            def _():
-                for h in range(2):
-                    send_ref[2 * chip + h, pl.ds(full_slots * row_count, half), :] = stage[
-                        r, pl.ds(h * half, half), columns
-                    ]
-
+        for h in range(2):
+            target = jnp.where(shared, owner - lax.rem(owner, 2) + h, owner)
+            start = jnp.where(shared, full_slots * row_count, slot * row_count + h * half)
+            send_ref[target, pl.ds(pl.multiple_of(start, half), half), :] = stage[
+                r, h * half : (h + 1) * half, columns
+            ]
+        partner = owner + 1 - 2 * lax.rem(owner, 2)
+        taken = table[partner * capacity + capacity - 1] >= 0
+        conflict_ref[0] = conflict_ref[0] | (shared & taken).astype(jnp.int32)
         table[owner * capacity + slot] = b
         if first_pass:
             total = jnp.zeros((8, LANES), jnp.float32)
@@ -110,7 +98,8 @@
     for r in range(block_rows):
         for load in loads[r]:
             load.wait()
-        lax.fori_loop(0, block_cols, lambda c, carry, r=r: (block(r, c), carry)[1], 0)
+        for c in range(block_cols):
+            block(r, c)
 
     for slot in range(capacity):
         info_ref[slot] = table[me * capacity + slot]
@@ -180,13 +169,12 @@
     return content.astype(jnp.bfloat16)
 
 
-def block_product(left_rows, grad, right_ready, right, times, put):
+def block_product(left_rows, grad, right, times, put):
     count = times.shape[0] // TILE
     for m in range(count):
         times[m * TILE : (m + 1) * TILE, :] = jnp.dot(
             left_rows(m), grad(), preferred_element_type=jnp.float32
         ).astype(jnp.bfloat16)
-    right_ready()
     total = jnp.zeros((8, times.shape[1]), jnp.float32)
     for m in range(count):
         value = jnp.dot(
@@ -198,53 +186,16 @@
 
 
 def multiply_kernel(
-    slot_count, final, info_ref, sums_ref, recv_ref, left_ref, right_ref,
-    out_ref, squares_ref, left_half, right_third, left, right, times, left_sems, right_sems, third_sems,
+    slot_count, final, info_ref, sums_ref, recv_ref, left_ref, right_ref, out_ref, squares_ref, times
 ):
-    _, group_size, row_halves, _, block_size = left.shape
+    _, group_size, row_halves, _, block_size = left_ref.shape
     row_count = row_halves * SUBLANES
-    tile_count = block_size // TILE
     per_tile = TILE // row_count
     lane_tiles = block_size // LANES
-    capacity = left_ref.shape[0]
-
-    def left_load(s, m):
-        rows = pl.ds(m * per_tile, per_tile)
-        return pltpu.make_async_copy(left_ref.at[s, rows], left.at[s, rows], left_sems.at[s, m])
-
-    def right_load(s):
-        return pltpu.make_async_copy(right_ref.at[s], right.at[s], right_sems.at[s])
-
-    for s in range(slot_count):
-        @pl.when(info_ref[s] >= 0)
-        def _():
-            for m in range(tile_count):
-                left_load(s, m).start()
-            right_load(s).start()
-
-    if not final:
-        last = capacity - 1
-        own, core = info_ref[last], info_ref[capacity + 1]
-
-        def third_loads():
-            return (
-                pltpu.make_async_copy(left_ref.at[last, :, core], left_half, third_sems.at[0]),
-                pltpu.make_async_copy(right_ref.at[last], right_third, third_sems.at[1]),
-            )
-
-        @pl.when(own >= 0)
-        def _():
-            for load in third_loads():
-                load.start()
-
     lane = lax.broadcasted_iota(jnp.int32, (1, LANES), 1)
     squares = jnp.zeros((1, LANES), jnp.float32)
     for s in range(slot_count):
         def compute(s=s):
-            def left_rows(m):
-                left_load(s, m).wait()
-                return left[s, m * per_tile : (m + 1) * per_tile].reshape(TILE, block_size)
-
             def put(m, tile):
                 for j in range(lane_tiles):
                     part = tile[:, j * LANES : (j + 1) * LANES].reshape(
@@ -256,12 +207,11 @@
                         ] = part[:, h]
 
             return block_product(
-                left_rows,
+                lambda m: left_ref[s, m * per_tile : (m + 1) * per_tile].reshape(TILE, block_size),
                 lambda: recv_ref[:, s * row_count : (s + 1) * row_count, :].reshape(
                     block_size, block_size
                 ),
-                lambda: right_load(s).wait(),
-                lambda: right[s],
+                lambda: right_ref[s],
                 times,
                 put,
             )
@@ -269,45 +219,30 @@
         value = lax.cond(info_ref[s] >= 0, compute, lambda: jnp.zeros((1, 1), jnp.float32))
         squares = squares + jnp.where(lane == info_ref[s], value, 0.0)
     squares_ref[...] = squares
-
     if final:
         out_ref[:, out_ref.shape[1] - 1] = jnp.broadcast_to(
             extra_tile(sums_ref[...], squares)[None], (group_size, SUBLANES, LANES)
         )
-    else:
-        @pl.when(own >= 0)
-        def _():
-            for load in third_loads():
-                load.wait()
 
 
 def multiply(info, sums, received, left_set, rights, slot_count, total_tiles, final):
-    capacity, group_size, row_halves, _, block_size = left_set.shape
+    _, group_size, _, _, block_size = left_set.shape
     return pl.pallas_call(
         functools.partial(multiply_kernel, slot_count, final),
         out_shape=(
             pltpu.VMEM((group_size, total_tiles, SUBLANES, LANES), jnp.bfloat16),
             jax.ShapeDtypeStruct((1, LANES), jnp.float32),
-            pltpu.VMEM((group_size, SUBLANES, block_size), jnp.bfloat16),
-            pltpu.VMEM((block_size, block_size), jnp.bfloat16),
-        ),
-        in_specs=[IN_SMEM, IN_VMEM, IN_VMEM, IN_ANY, IN_ANY],
-        out_specs=(IN_VMEM,) * 4,
-        scratch_shapes=[
-            pltpu.VMEM((slot_count, group_size, row_halves, SUBLANES, block_size), jnp.bfloat16),
-            pltpu.VMEM((slot_count, block_size, block_size), jnp.bfloat16),
-            pltpu.VMEM((block_size, block_size), jnp.bfloat16),
-            pltpu.SemaphoreType.DMA((slot_count, block_size // TILE)),
-            pltpu.SemaphoreType.DMA((slot_count,)),
-            pltpu.SemaphoreType.DMA((2,)),
-        ],
-        compiler_params=pltpu.CompilerParams(vmem_limit_bytes=(36 if final else 26) * 2**20),
+        ),
+        in_specs=[IN_SMEM] + [IN_VMEM] * 4,
+        out_specs=(IN_VMEM, IN_VMEM),
+        scratch_shapes=[pltpu.VMEM((block_size, block_size), jnp.bfloat16)],
+        compiler_params=pltpu.CompilerParams(vmem_limit_bytes=12 * 2**20),
         cost_estimate=pl.CostEstimate(
             flops=slot_count * 4 * block_size**3,
             bytes_accessed=slot_count * 8 * block_size**2,
             transcendentals=0,
         ),
-    )(info, sums, *keep_vmem(received), *keep_hbm(left_set, rights))
+    )(info, sums, *keep_vmem(received, left_set, rights))
 
 
 def shared_kernel(
@@ -352,7 +287,6 @@
         return block_product(
             lambda m: left_from[m * per_tile : (m + 1) * per_tile].reshape(TILE, block_size),
             lambda: grad[...].reshape(block_size, block_size),
-            lambda: None,
             lambda: right_from[...],
             times,
             put,
@@ -360,7 +294,7 @@
 
     value = lax.cond(
         info_ref[capacity - 1] >= 0,
-        lambda: compute(left_ref, right_ref),
+        lambda: compute(left_ref.at[capacity - 1, :, core], right_ref.at[capacity - 1]),
         lambda: lax.cond(
             block >= 0,
             lambda: compute(left_away, right_away),
@@ -384,7 +318,7 @@
 
 
 def multiply_shared(
-    info, sums, squares, own, other, left_half, right, left_away, right_away, outgoing
+    info, sums, squares, own, other, left_set, rights, left_away, right_away, outgoing
 ):
     group_size, half, block_size = own.shape
     lane_tiles = block_size // LANES
@@ -404,13 +338,13 @@
             pltpu.SemaphoreType.DMA((rows // TILE,)),
             pltpu.SemaphoreType.DMA,
         ],
-        compiler_params=pltpu.CompilerParams(vmem_limit_bytes=32 * 2**20),
+        compiler_params=pltpu.CompilerParams(vmem_limit_bytes=14 * 2**20),
         cost_estimate=pl.CostEstimate(
             flops=4 * rows * block_size**2, bytes_accessed=8 * rows * block_size, transcendentals=0
         ),
     )(
         info, sums, squares,
-        *keep_vmem(own, other, left_half, right, left_away, right_away, outgoing),
+        *keep_vmem(own, other, left_set, rights, left_away, right_away, outgoing),
     )
 
 
@@ -512,11 +446,11 @@
         other = lax.ppermute(own, "dp", partner)
         left_away = lax.ppermute(left_away, "dp", partner)
         right_away = lax.ppermute(right_away, "dp", partner)
-        outgoing, squares, left_half, right_third = multiply(
+        outgoing, squares = multiply(
             info, sums, received, left_set, rights, full, full * slot_tiles + lane_tiles + 1, False,
         )
         outgoing = multiply_shared(
-            info, sums, squares, own, other, left_half, right_third, left_away, right_away, outgoing
+            info, sums, squares, own, other, left_set, rights, left_away, right_away, outgoing
         )
         return unpack(owners, slots, exchange(outgoing), gradient.shape, full)
 

time: 168 us -> 164 us (0.976)
  Pallas kernels: 25.1 us -> 16.3 us
  blocking collectives: 140 us -> 145 us
    pallas_call x1, Pallas kernels: 12.3 us -> 5.27 us  [multiply(): pl.pallas_call(functools.partial(multiply_kernel, slot_count, final), out...]
    all_to_all x2, blocking collectives: 140 us -> 145 us  [exchange(): return lax.all_to_all(value, 'dp', split_axis=0, concat_axis=0, tiled=True)]
    pallas_call x1, Pallas kernels: 9.49 us -> 7.72 us  [pack(): pl.pallas_call(functools.partial(pack_kernel, full_slots, capacity, first...]
  transfers between devices with their start and end apart: 3 -> 3, of which waited for: 0 -> 1; matrix products, arithmetic and copies ran while one was open for 0% -> 0% of each run, Pallas kernels for 7% -> 3%
where the time goes in v3:
time: 164 us
  blocking collectives  145 us (88%)
  Pallas kernels  16.3 us (10%)
    all_to_all x2, blocking collectives, exchange(): return lax.all_to_all(value, 'dp', split_axis=0, concat_axis=0, tiled=True)  145 us
    pallas_call x1, Pallas kernels, pack(): pl.pallas_call(functools.partial(pack_kernel, full_slots, capacity, first...  7.72 us
    pallas_call x1, Pallas kernels, multiply(): pl.pallas_call(functools.partial(multiply_kernel, slot_count, final), out...  5.27 us
  transfers between devices with their start and end apart: 3, of which 1 were waited for; matrix products, arithmetic and copies ran while one was open for 0% of the time, Pallas kernels for 3%

profile of v3, /device:TPU:1, one launch (start us, length us, event | category | flops | bytes accessed | tf_op | source)
XLA Modules:
  0.0 164.5 jit_solution(18325242241875340942)
XLA Ops:
  0.0 0.0 copy-start
  0.0 0.0 copy-start.3
  0.0 0.0 copy-start.6
  0.0 7.7 %shard_map.57 = (bf16[32,80,1024]{2,1,0:T(8,128)(2,1)S(1)}, f32[1,128]{1,0:T(1,128)S(1)}, s32[56]{0:T(128)S(1)}, s32[5]{0:T(128)S(1)}, s32[1]{0:T(128)}, /*index...) custom-call(s32[1]{0:T(128)} %bitcast.me_ref, s32[56]{0:T(128)} %bitcast.11, bf16[8,32,7168]{2,1,0:T(8,128)(2,1)} %grad_ref.1, ...), custom_call_target="tpu_custom_call" | custom-call | flops 18350080 | bytes 14680064 | tf_op jit(solution)/shard_map/pallas_call | solution.py:123
  8.4 0.0 copy-done
  8.4 0.0 copy-done.3
  8.4 0.0 copy-done.6
  8.4 155.9 %conditional.1 = (bf16[8,32,7168]{2,1,0:T(8,128)(2,1)}) conditional(s32[]{:T(128)} %bitcast.4, (bf16[32,80,1024]{2,1,0:T(8,128)(2,1)S(1)}, bf16[32,16,1024]{2,1,0:T(8,128)(2,1)S(1)}, bf16[1024,1024]{1,0:T(8,128)(2,1)S(1)}, s32[5]{0:T(128)S(1)}, f32[1,128]{1,0:T(1,128)S(1)}, /*index=5*/bf16[3,32,2,16,1024]{4,3,2,1,0:T(8,128)(2,1)S(1)}, ...), branch_computations={%region_0.0_spmd, %region_1.0_spmd} | conditional | flops 12905086976 | bytes 173277312 | solution.py:457
  8.4 70.5 %all_to_all.16.recv_ref = bf16[32,80,1024]{2,1,0:T(8,128)(2,1)S(1)} all-to-all(bf16[32,80,1024]{2,1,0:T(8,128)(2,1)S(1)} %get-tuple-element.46), channel_id=1, replica_groups=mesh['dp'=32,'mp'=4] {'dp'}, dimensions={0} | all-to-all | bytes 10485760 | tf_op jit(solution)/shard_map/cond/branch_0_fun/all_to_all | solution.py:410
  78.9 0.4 collective-permute-start.2
  79.3 0.1 slice.2.own_ref
  79.4 0.2 collective-permute-start
  79.6 0.4 collective-permute-start.1
  80.0 5.3 %branch_0_fun.3 = (bf16[32,41,16,128]{3,2,1,0:T(8,128)(2,1)S(1)}, f32[1,128]{1,0:T(1,128)S(1)}) custom-call(s32[5]{0:T(128)S(1)} %get-tuple-element.44.info_ref, f32[1,128]{1,0:T(1,128)S(1)} %get-tuple-element.45.sums_ref, bf16[32,80,1024]{2,1,0:T(8,128)(2,1)S(1)} %all_to_all.16.recv_ref, bf16[3,32,2,16,1024]{4,3,2,1,0:T(8,128)(2,1)S(1)} %get-tuple-element.50.left_ref, ...), custom_call_target="tpu_custom_call" | custom-call | flops 8589934592 | bytes 16777216 | tf_op jit(solution)/shard_map/cond/branch_0_fun/pallas_call | solution.py:230
  85.3 0.0 collective-permute-done.other_ref
  85.3 0.8 collective-permute-done.1.left_away
  86.1 0.0 collective-permute-done.2.right_away
  86.1 0.6 branch_0_fun.4
  86.8 74.6 %all_to_all.17.back_ref = bf16[32,41,16,128]{3,2,1,0:T(8,128)(2,1)S(1)} all-to-all(bf16[32,41,16,128]{3,2,1,0:T(8,128)(2,1)S(1)} %branch_0_fun.4), channel_id=1, replica_groups=mesh['dp'=32,'mp'=4] {'dp'}, dimensions={0} | all-to-all | bytes 10747904 | tf_op jit(solution)/shard_map/cond/branch_0_fun/all_to_all | solution.py:410
  161.4 2.7 %branch_0_fun.5 = bf16[8,32,7168]{2,1,0:T(8,128)(2,1)} custom-call(s32[56]{0:T(128)S(1)} %get-tuple-element.42.owner_ref, s32[56]{0:T(128)S(1)} %get-tuple-element.43.slot_ref, bf16[32,41,16,128]{3,2,1,0:T(8,128)(2,1)S(1)} %all_to_all.17.back_ref), custom_call_target="tpu_custom_call" | custom-call | flops 1835008 | bytes 7340032 | tf_op jit(solution)/shard_map/cond/branch_0_fun/pallas_call | solution.py:391
Async XLA Ops:
  0.0 8.4 %copy-start = (bf16[1,1,3,1024,1024]{4,3,2,1,0:T(8,128)(2,1)S(1)}, bf16[1,1,3,1024,1024]{4,3,2,1,0:T(8,128)(2,1)}, u32[]{:S(2)}) copy-start(bf16[1,1,3,1024,1024]{4,3,2,1,0:T(8,128)(2,1)} %param.10) | copy-start | bytes 18874372
  0.0 8.4 %copy-start.3 = (bf16[1,1,3,1024,1024]{4,3,2,1,0:T(8,128)(2,1)S(1)}, bf16[1,1,3,1024,1024]{4,3,2,1,0:T(8,128)(2,1)}, u32[]{:S(2)}) copy-start(bf16[1,1,3,1024,1024]{4,3,2,1,0:T(8,128)(2,1)} %param.11) | copy-start | bytes 18874372
  0.0 8.4 %copy-start.6 = (s32[56,1]{0,1:T(1,128)S(1)}, s32[56,1]{0,1:T(1,128)}, u32[]{:S(2)}) copy-start(s32[56,1]{0,1:T(1,128)} %param.9) | copy-start | bytes 676
  78.9 7.2 %collective-permute-start.2 = (bf16[1024,1024]{1,0:T(8,128)(2,1)S(1)}, bf16[1024,1024]{1,0:T(8,128)(2,1)S(1)}, u32[]{:S(2)}, u32[]{:S(2)}) collective-permute-start(bf16[1024,1024]{1,0:T(8,128)(2,1)S(1)} %get-tuple-element.54), channel_id=1, source_target_pairs={{0,4},{4,0},{8,12},{12,8},{16,20},{20,16},{24,28},{28,24},{32,36},... | collective-permute-start | bytes 6291464 | tf_op jit(solution)/shard_map/cond/branch_0_fun/ppermute | solution.py:448
  79.4 5.9 %collective-permute-start = (bf16[32,16,1024]{2,1,0:T(8,128)(2,1)S(1)}, bf16[32,16,1024]{2,1,0:T(8,128)(2,1)S(1)}, u32[]{:S(2)}, u32[]{:S(2)}) collective-permute-start(bf16[32,16,1024]{2,1,0:T(8,128)(2,1)S(1)} %slice.2.own_ref), channel_id=1, source_target_pairs={{0,4},{4,0},{8,12},{12,8},{16,20},{20,16},{24,28},{28,24},{32,36},... | collective-permute-start | bytes 3145736 | tf_op jit(solution)/shard_map/cond/branch_0_fun/ppermute | solution.py:446
  79.6 6.5 %collective-permute-start.1 = (bf16[32,16,1024]{2,1,0:T(8,128)(2,1)S(1)}, bf16[32,16,1024]{2,1,0:T(8,128)(2,1)S(1)}, u32[]{:S(2)}, u32[]{:S(2)}) collective-permute-start(bf16[32,16,1024]{2,1,0:T(8,128)(2,1)S(1)} %get-tuple-element.53), channel_id=1, source_target_pairs={{0,4},{4,0},{8,12},{12,8},{16,20},{20,16},{24,28},{28,24},{32,36},... | collective-permute-start | bytes 3145736 | tf_op jit(solution)/shard_map/cond/branch_0_fun/ppermute | solution.py:447

commit v4 on v3

--- a/solution.py
+++ b/solution.py
@@ -247,42 +247,26 @@
 
 def shared_kernel(
     info_ref, sums_ref, squares_ref, own_ref, other_ref, left_ref, right_ref, left_away, right_away,
-    before_ref, out_ref,
-    grad, times, product, extra, grad_sems, out_sems, extra_sem,
+    before_ref, out_ref, grad, times,
 ):
     group_size, _, half, block_size = grad.shape
-    tile_count = times.shape[0] // TILE
     per_tile = TILE // half
-    lane_tiles = product.shape[1]
+    lane_tiles = block_size // LANES
     first_tile = out_ref.shape[1] - 1 - lane_tiles
     capacity = info_ref.shape[0] - 2
     block = jnp.maximum(info_ref[capacity - 1], info_ref[capacity])
     core = info_ref[capacity + 1]
     del before_ref
-    loads = [
-        pltpu.make_async_copy(own_ref, grad.at[:, core], grad_sems.at[0]),
-        pltpu.make_async_copy(other_ref, grad.at[:, 1 - core], grad_sems.at[1]),
-    ]
-
-    def store(m):
-        return pltpu.make_async_copy(
-            product.at[pl.ds(m * per_tile, per_tile)],
-            out_ref.at[pl.ds(m * per_tile, per_tile), pl.ds(first_tile, lane_tiles)],
-            out_sems.at[m],
-        )
 
     def compute(left_from, right_from):
-        for load in loads:
-            load.start()
-        for load in loads:
-            load.wait()
+        grad[:, pl.ds(core, 1)] = own_ref[...][:, None]
+        grad[:, pl.ds(1 - core, 1)] = other_ref[...][:, None]
 
         def put(m, tile):
             for j in range(lane_tiles):
-                product[m * per_tile : (m + 1) * per_tile, j] = tile[
+                out_ref[m * per_tile : (m + 1) * per_tile, first_tile + j] = tile[
                     :, j * LANES : (j + 1) * LANES
                 ].reshape(per_tile, SUBLANES, LANES)
-            store(m).start()
 
         return block_product(
             lambda m: left_from[m * per_tile : (m + 1) * per_tile].reshape(TILE, block_size),
@@ -303,40 +287,25 @@
     )
     lane = lax.broadcasted_iota(jnp.int32, (1, LANES), 1)
     squares = squares_ref[...] + jnp.where(lane == block, value, 0.0)
-    extra[...] = jnp.broadcast_to(extra_tile(sums_ref[...], squares)[None, None], extra.shape)
-    send_extra = pltpu.make_async_copy(
-        extra, out_ref.at[:, pl.ds(out_ref.shape[1] - 1, 1)], extra_sem
-    )
-    send_extra.start()
-
-    @pl.when(block >= 0)
-    def _():
-        for m in range(tile_count):
-            store(m).wait()
-
-    send_extra.wait()
+    out_ref[:, out_ref.shape[1] - 1] = jnp.broadcast_to(
+        extra_tile(sums_ref[...], squares)[None], (group_size, SUBLANES, LANES)
+    )
 
 
 def multiply_shared(
     info, sums, squares, own, other, left_set, rights, left_away, right_away, outgoing
 ):
     group_size, half, block_size = own.shape
-    lane_tiles = block_size // LANES
     rows = group_size * half
     return pl.pallas_call(
         shared_kernel,
         out_shape=pltpu.VMEM(outgoing.shape, outgoing.dtype),
-        in_specs=[IN_SMEM, IN_VMEM, IN_VMEM, IN_ANY, IN_ANY] + [IN_VMEM] * 4 + [IN_ANY],
-        out_specs=IN_ANY,
+        in_specs=[IN_SMEM] + [IN_VMEM] * 9,
+        out_specs=IN_VMEM,
         input_output_aliases={9: 0},
         scratch_shapes=[
             pltpu.VMEM((group_size, 2, half, block_size), jnp.bfloat16),
             pltpu.VMEM((rows, block_size), jnp.bfloat16),
-            pltpu.VMEM((group_size, lane_tiles, SUBLANES, LANES), jnp.bfloat16),
-            pltpu.VMEM((group_size, 1, SUBLANES, LANES), jnp.bfloat16),
-            pltpu.SemaphoreType.DMA((2,)),
-            pltpu.SemaphoreType.DMA((rows // TILE,)),
-            pltpu.SemaphoreType.DMA,
         ],
         compiler_params=pltpu.CompilerParams(vmem_limit_bytes=14 * 2**20),
         cost_estimate=pl.CostEstimate(

time: 164 us -> 163 us (level)
  blocking collectives: 145 us -> 141 us
  Pallas kernels: 16.3 us -> 18.8 us
    all_to_all x2, blocking collectives: 145 us -> 141 us  [exchange(): return lax.all_to_all(value, 'dp', split_axis=0, concat_axis=0, tiled=True)]
    pallas_call x1, Pallas kernels: 0.64 us -> 3.14 us  [multiply_shared(): pl.pallas_call(shared_kernel, out_shape=pltpu.VMEM(outgoing.shape, outgoi...]
where the time goes in v4:
time: 163 us
  blocking collectives  141 us (87%)
  Pallas kernels  18.8 us (12%)
    all_to_all x2, blocking collectives, exchange(): return lax.all_to_all(value, 'dp', split_axis=0, concat_axis=0, tiled=True)  141 us
    pallas_call x1, Pallas kernels, pack(): pl.pallas_call(functools.partial(pack_kernel, full_slots, capacity, first...  7.72 us
    pallas_call x1, Pallas kernels, multiply(): pl.pallas_call(functools.partial(multiply_kernel, slot_count, final), out...  5.27 us
  transfers between devices with their start and end apart: 3, of which 1 were waited for; matrix products, arithmetic and copies ran while one was open for 0% of the time, Pallas kernels for 3%

profile of v4, /device:TPU:1, one launch (start us, length us, event | category | flops | bytes accessed | tf_op | source)
XLA Modules:
  0.0 162.9 jit_solution(4140560843912809600)
XLA Ops:
  0.0 0.0 copy-start
  0.0 0.0 copy-start.3
  0.0 0.0 copy-start.6
  0.0 7.7 %shard_map.57 = (bf16[32,80,1024]{2,1,0:T(8,128)(2,1)S(1)}, f32[1,128]{1,0:T(1,128)S(1)}, s32[56]{0:T(128)S(1)}, s32[5]{0:T(128)S(1)}, s32[1]{0:T(128)}, /*index...) custom-call(s32[1]{0:T(128)} %bitcast.me_ref, s32[56]{0:T(128)} %bitcast.11, bf16[8,32,7168]{2,1,0:T(8,128)(2,1)} %grad_ref.1, ...), custom_call_target="tpu_custom_call" | custom-call | flops 18350080 | bytes 14680064 | tf_op jit(solution)/shard_map/pallas_call | solution.py:123
  8.4 0.0 copy-done
  8.4 0.0 copy-done.3
  8.4 0.0 copy-done.6
  8.4 154.3 %conditional.1 = (bf16[8,32,7168]{2,1,0:T(8,128)(2,1)}) conditional(s32[]{:T(128)} %bitcast.4, (bf16[32,80,1024]{2,1,0:T(8,128)(2,1)S(1)}, bf16[32,16,1024]{2,1,0:T(8,128)(2,1)S(1)}, bf16[1024,1024]{1,0:T(8,128)(2,1)S(1)}, s32[5]{0:T(128)S(1)}, f32[1,128]{1,0:T(1,128)S(1)}, /*index=5*/bf16[3,32,2,16,1024]{4,3,2,1,0:T(8,128)(2,1)S(1)}, ...), branch_computations={%region_0.0_spmd, %region_1.0_spmd} | conditional | flops 12905086976 | bytes 173277312 | solution.py:426
  8.4 70.5 %all_to_all.16.recv_ref = bf16[32,80,1024]{2,1,0:T(8,128)(2,1)S(1)} all-to-all(bf16[32,80,1024]{2,1,0:T(8,128)(2,1)S(1)} %get-tuple-element.46), channel_id=1, replica_groups=mesh['dp'=32,'mp'=4] {'dp'}, dimensions={0} | all-to-all | bytes 10485760 | tf_op jit(solution)/shard_map/cond/branch_0_fun/all_to_all | solution.py:379
  78.9 0.4 collective-permute-start.2
  79.3 0.1 slice.2.own_ref
  79.4 0.2 collective-permute-start
  79.6 0.4 collective-permute-start.1
  80.0 5.3 %branch_0_fun.3 = (bf16[32,41,16,128]{3,2,1,0:T(8,128)(2,1)S(1)}, f32[1,128]{1,0:T(1,128)S(1)}) custom-call(s32[5]{0:T(128)S(1)} %get-tuple-element.44.info_ref, f32[1,128]{1,0:T(1,128)S(1)} %get-tuple-element.45.sums_ref, bf16[32,80,1024]{2,1,0:T(8,128)(2,1)S(1)} %all_to_all.16.recv_ref, bf16[3,32,2,16,1024]{4,3,2,1,0:T(8,128)(2,1)S(1)} %get-tuple-element.50.left_ref, ...), custom_call_target="tpu_custom_call" | custom-call | flops 8589934592 | bytes 16777216 | tf_op jit(solution)/shard_map/cond/branch_0_fun/pallas_call | solution.py:230
  85.3 0.0 collective-permute-done.other_ref
  85.3 0.8 collective-permute-done.1.left_away
  86.1 0.0 collective-permute-done.2.right_away
  86.1 3.1 %branch_0_fun.4 = bf16[32,41,16,128]{3,2,1,0:T(8,128)(2,1)S(1)} custom-call(s32[5]{0:T(128)S(1)} %get-tuple-element.44.info_ref, f32[1,128]{1,0:T(1,128)S(1)} %get-tuple-element.45.sums_ref, f32[1,128]{1,0:T(1,128)S(1)} %get-tuple-element.52.squares_ref, bf16[32,16,1024]{2,1,0:T(8,128)(2,1)S(1)} %slice.2.own_ref, ...), custom_call_target="tpu_custom_call", output_to_operand_aliasing={{}: (9, {})} | custom-call | flops 2147483648 | bytes 4194304 | tf_op jit(solution)/shard_map/cond/branch_0_fun/pallas_call | solution.py:300
  89.3 70.6 %all_to_all.17.back_ref = bf16[32,41,16,128]{3,2,1,0:T(8,128)(2,1)S(1)} all-to-all(bf16[32,41,16,128]{3,2,1,0:T(8,128)(2,1)S(1)} %branch_0_fun.4), channel_id=1, replica_groups=mesh['dp'=32,'mp'=4] {'dp'}, dimensions={0} | all-to-all | bytes 10747904 | tf_op jit(solution)/shard_map/cond/branch_0_fun/all_to_all | solution.py:379
  159.8 2.7 %branch_0_fun.5 = bf16[8,32,7168]{2,1,0:T(8,128)(2,1)} custom-call(s32[56]{0:T(128)S(1)} %get-tuple-element.42.owner_ref, s32[56]{0:T(128)S(1)} %get-tuple-element.43.slot_ref, bf16[32,41,16,128]{3,2,1,0:T(8,128)(2,1)S(1)} %all_to_all.17.back_ref), custom_call_target="tpu_custom_call" | custom-call | flops 1835008 | bytes 7340032 | tf_op jit(solution)/shard_map/cond/branch_0_fun/pallas_call | solution.py:360
Async XLA Ops:
  0.0 8.4 %copy-start = (bf16[1,1,3,1024,1024]{4,3,2,1,0:T(8,128)(2,1)S(1)}, bf16[1,1,3,1024,1024]{4,3,2,1,0:T(8,128)(2,1)}, u32[]{:S(2)}) copy-start(bf16[1,1,3,1024,1024]{4,3,2,1,0:T(8,128)(2,1)} %param.10) | copy-start | bytes 18874372
  0.0 8.4 %copy-start.3 = (bf16[1,1,3,1024,1024]{4,3,2,1,0:T(8,128)(2,1)S(1)}, bf16[1,1,3,1024,1024]{4,3,2,1,0:T(8,128)(2,1)}, u32[]{:S(2)}) copy-start(bf16[1,1,3,1024,1024]{4,3,2,1,0:T(8,128)(2,1)} %param.11) | copy-start | bytes 18874372
  0.0 8.4 %copy-start.6 = (s32[56,1]{0,1:T(1,128)S(1)}, s32[56,1]{0,1:T(1,128)}, u32[]{:S(2)}) copy-start(s32[56,1]{0,1:T(1,128)} %param.9) | copy-start | bytes 676
  78.9 7.2 %collective-permute-start.2 = (bf16[1024,1024]{1,0:T(8,128)(2,1)S(1)}, bf16[1024,1024]{1,0:T(8,128)(2,1)S(1)}, u32[]{:S(2)}, u32[]{:S(2)}) collective-permute-start(bf16[1024,1024]{1,0:T(8,128)(2,1)S(1)} %get-tuple-element.54), channel_id=1, source_target_pairs={{0,4},{4,0},{8,12},{12,8},{16,20},{20,16},{24,28},{28,24},{32,36},... | collective-permute-start | bytes 6291464 | tf_op jit(solution)/shard_map/cond/branch_0_fun/ppermute | solution.py:417
  79.4 5.9 %collective-permute-start = (bf16[32,16,1024]{2,1,0:T(8,128)(2,1)S(1)}, bf16[32,16,1024]{2,1,0:T(8,128)(2,1)S(1)}, u32[]{:S(2)}, u32[]{:S(2)}) collective-permute-start(bf16[32,16,1024]{2,1,0:T(8,128)(2,1)S(1)} %slice.2.own_ref), channel_id=1, source_target_pairs={{0,4},{4,0},{8,12},{12,8},{16,20},{20,16},{24,28},{28,24},{32,36},... | collective-permute-start | bytes 3145736 | tf_op jit(solution)/shard_map/cond/branch_0_fun/ppermute | solution.py:415
  79.6 6.5 %collective-permute-start.1 = (bf16[32,16,1024]{2,1,0:T(8,128)(2,1)S(1)}, bf16[32,16,1024]{2,1,0:T(8,128)(2,1)S(1)}, u32[]{:S(2)}, u32[]{:S(2)}) collective-permute-start(bf16[32,16,1024]{2,1,0:T(8,128)(2,1)S(1)} %get-tuple-element.53), channel_id=1, source_target_pairs={{0,4},{4,0},{8,12},{12,8},{16,20},{20,16},{24,28},{28,24},{32,36},... | collective-permute-start | bytes 3145736 | tf_op jit(solution)/shard_map/cond/branch_0_fun/ppermute | solution.py:416
